TPU v7x, 128 devices: a whole 4x4x4 slice. The times are simulated.
128 devices in a mesh: mp: 2 (over core), tile: 64 (over y, x, z).
Axes of the slice: x: 4, y: 4, z: 4, core: 2. Of those that a mesh axis runs over, the one named last changes fastest.
Arguments:
- breeze_vectors: float32 [2, 65536], P(None, ('mp', 'tile')), may hold values from -60 to 60
- prior_drag_height: float32 [65536], P(('mp', 'tile')), may hold values from 0.0001 to 0.003
- prior_skin_heat_anomaly: float32 [65536], P(('mp', 'tile')), may hold values from -6 to 6
- sea_flow_vectors: float32 [2, 1024, 256], P(None, ('mp', 'tile')), may hold values from -4 to 4
- skin_heat_anomaly: float32 [1024, 256], P(('mp', 'tile')), may hold values from -6 to 6
- subsurface_heat_anomaly: float32 [1024, 256], P(('mp', 'tile')), may hold values from -4 to -1
- swell_density_table: float32 [36, 32, 1024, 256], P(None, None, ('mp', 'tile')), may hold values from 0.01 to 1
- marine_indicator_grid: int32 [1024, 256], P(('mp', 'tile')), may hold values from 0 to 1, as said below
- home_air_provider: int32 [128, 4608], P(('mp', 'tile')), may hold values from 0 to 511
- home_grid_receiver: int32 [128, 4608], P(('mp', 'tile')), may hold values from 0 to 2047
- flooded_share_factor: float32 [128, 4608], P(('mp', 'tile'))
- border_air_provider: int32 [128, 384], P(('mp', 'tile')), may hold values from 0 to 511
- border_grid_receiver: int32 [128, 384], P(('mp', 'tile')), may hold values from 0 to 2047
- border_share_factor: float32 [128, 384], P(('mp', 'tile'))
- active_couple_tally: int32 [128, 2], P(('mp', 'tile')), may hold values from 0 to 4213, as said below
Outputs:
- currents_out: float32 [2, 1024, 256], P(None, ('mp', 'tile'))
- sst_out: float32 [1024, 256], P(('mp', 'tile'))
- spectrum_out: float32 [36, 32, 1024, 256], P(None, None, ('mp', 'tile'))
- air_drag_height_tenths: float32 [65536], P(('mp', 'tile'))
- air_heat_anomaly_back: float32 [65536], P(('mp', 'tile'))
Inputs may be any that keep to these rules, and one draw needn't show every extreme that they name: `marine_indicator_grid`: 1 on every row below 768 and on every row from 896 on; in each column the land, if any, is one run that ends at row 895. Live slots come first in each list. active_couple_tally[0, 0] = 0. active_couple_tally[d, 0] is at most 383 and active_couple_tally[d, 1] at most (383) * 11; both are reached for some d.
All inputs are finite; a program needn't handle non-finite values.
Results may differ from a plain program's by a relative error of at most 0.0001.
Values sent between devices are 32-bit elements; how exact they have to be, the bound alone decides.
A program may use at most 128 MiB of HBM per device.

v0:
```python
import math

import jax
import jax.numpy as jnp
from jax import lax
from jax.sharding import PartitionSpec as P

WSTEPS = 4
OSTEPS = 4


GRAV = 9.81


def padded(cells, sides, width):
    for axis, dim in sides:
        count = lax.axis_size(axis)
        ends = count - 1
        head = lax.slice_in_dim(cells, 0, width, axis=dim)
        tail = lax.slice_in_dim(cells, cells.shape[dim] - width, cells.shape[dim], axis=dim)
        cells = jnp.concatenate(
            [
                lax.ppermute(tail, axis, [(i, (i + 1) % count) for i in range(ends)]),
                cells,
                lax.ppermute(head, axis, [((i + 1) % count, i) for i in range(ends)]),
            ],
            axis=dim,
        )
    return cells


def passed_along(value, axis, by):
    peers = lax.axis_size(axis)
    pairs = [(i, i + by) for i in range(peers) if 0 <= i + by < peers]
    return lax.ppermute(value, axis, pairs)


def spectral_tables(ndir, nfreq):
    angles = (jnp.arange(ndir, dtype=jnp.float32) + 0.5) * (2.0 * math.pi / ndir)
    frequency = 0.04 * jnp.power(jnp.float32(1.1), jnp.arange(nfreq, dtype=jnp.float32))
    cos_table = jnp.cos(angles)[:, None, None, None]
    sin_table = jnp.sin(angles)[:, None, None, None]
    speeds = (GRAV / (2.0 * math.pi * frequency))[None, :, None, None]
    courant = (0.028 / frequency)[None, :, None, None]
    bin_width = (0.1 * frequency * (2.0 * math.pi / ndir))[None, :, None, None]
    return (cos_table, sin_table, speeds, courant, bin_width)


def advect(swell_power_density, haloed_lines, tables):
    cos_table, sin_table, speeds, courant, bin_width = tables
    zero_column = jnp.zeros(swell_power_density.shape[:3] + (1,), swell_power_density.dtype)
    columns = jnp.concatenate([zero_column, swell_power_density, zero_column], axis=3)
    east_pos = courant * jnp.maximum(cos_table, 0.0)
    east_neg = courant * jnp.maximum(-cos_table, 0.0)
    north_pos = courant * jnp.maximum(sin_table, 0.0)
    north_neg = courant * jnp.maximum(-sin_table, 0.0)
    return (
        swell_power_density
        - east_pos * (swell_power_density - columns[..., :-2])
        - east_neg * (swell_power_density - columns[..., 2:])
        - north_pos * (swell_power_density - haloed_lines[:, :, :-2])
        - north_neg * (swell_power_density - haloed_lines[:, :, 2:])
    )


def wave_source(advected, wind_east, wind_north, marine_indicator, tables):
    cos_table, sin_table, speeds, courant, bin_width = tables
    energy_sum = jnp.sum(advected * bin_width, axis=(0, 1))
    damping = 0.3 * energy_sum / (energy_sum + 1.0)
    wind_along = cos_table * wind_east + sin_table * wind_north
    growth = 0.01 * jnp.maximum(wind_along / speeds - 1.0, 0.0)
    return advected * (1.0 + growth - damping) * marine_indicator


def marine_advance(
    marine_variable_bundle,
    haloed_lines,
    driving_input,
    drag_damping,
    subsurface_heat_anomaly,
    marine_indicator,
):
    columns = jnp.pad(marine_variable_bundle, ((0, 0), (0, 0), (1, 1)))
    diffusion_operator = (
        haloed_lines[:, 2:]
        + haloed_lines[:, :-2]
        + columns[:, :, 2:]
        + columns[:, :, :-2]
        - 4.0 * marine_variable_bundle
    )
    east_flow = marine_variable_bundle[0]
    north_flow = marine_variable_bundle[1]
    heat_anomaly = marine_variable_bundle[2]
    new_east = marine_indicator * (
        east_flow
        + 0.1 * driving_input[0]
        + 0.2 * north_flow
        - 0.05 * east_flow
        + 0.2 * diffusion_operator[0]
    )
    new_north = marine_indicator * (
        north_flow
        + 0.1 * driving_input[1]
        - 0.2 * east_flow
        - 0.05 * north_flow
        + 0.2 * diffusion_operator[1]
    )
    updated_heat_anomaly = marine_indicator * (
        heat_anomaly
        + 0.2 * diffusion_operator[2]
        - 0.05 * drag_damping * (heat_anomaly - subsurface_heat_anomaly)
    )
    return jnp.stack([new_east, new_north, updated_heat_anomaly])


def atmosphere_forcing(breeze_vectors, prior_drag_height):
    drag_factor = (0.4 / jnp.log(10.0 / prior_drag_height)) ** 2
    speed = jnp.sqrt(
        breeze_vectors[0] * breeze_vectors[0] + breeze_vectors[1] * breeze_vectors[1] + 1.0
    )
    return jnp.stack(
        [
            1.2 * drag_factor * speed * breeze_vectors[0],
            1.2 * drag_factor * speed * breeze_vectors[1],
            breeze_vectors[0],
            breeze_vectors[1],
        ]
    )


def fine_roughness(swell_power_density, drag_damping, tables):
    bin_width = tables[4]
    wave_height = 4.0 * jnp.sqrt(jnp.sum(swell_power_density * bin_width, axis=(0, 1)) + 1e-06)
    return 1000.0 * ((0.011 + 0.02 * wave_height) * drag_damping / GRAV + 1.5e-05)


def one_hot(indices, width):
    return (indices[:, None] == jnp.arange(width, dtype=jnp.int32)[None, :]).astype(jnp.float32)


def precise_dot(left, right):
    return jnp.dot(left, right, precision=lax.Precision.HIGHEST, preferred_element_type=jnp.float32)


def remap_table(source_hot, target_hot):
    return lax.dot_general(
        source_hot,
        target_hot,
        (((0,), (0,)), ((), ())),
        precision=lax.Precision.HIGHEST,
        preferred_element_type=jnp.float32,
    )


def wave_rows(swell_power_density):
    return padded(swell_power_density, ((("mp", "tile"), 2),), 1)


def per_device(
    breeze_vectors,
    prior_drag_height,
    prior_skin_heat_anomaly,
    sea_flow_vectors,
    skin_heat_anomaly,
    subsurface_heat_anomaly,
    swell_density_table,
    marine_indicator_grid,
    home_air_provider,
    home_grid_receiver,
    flooded_share_factor,
    border_air_provider,
    border_grid_receiver,
    border_share_factor,
    active_couple_tally,
):
    tile_y_extent = skin_heat_anomaly.shape[0]
    tile_x_extent = skin_heat_anomaly.shape[1]
    fine_cells = tile_y_extent * tile_x_extent
    atmos_cells = prior_drag_height.shape[0]
    own_slots = home_air_provider.shape[1]
    edge_slots = border_air_provider.shape[1]
    forcing_atm = atmosphere_forcing(breeze_vectors, prior_drag_height)
    own_live = jnp.where(
        jnp.arange(own_slots, dtype=jnp.int32) < active_couple_tally[0, 1],
        flooded_share_factor[0],
        0.0,
    )
    edge_live = jnp.where(
        jnp.arange(edge_slots, dtype=jnp.int32) < active_couple_tally[0, 0],
        border_share_factor[0],
        0.0,
    )
    own_target = one_hot(home_grid_receiver[0], fine_cells) * own_live[:, None]
    own_table = remap_table(one_hot(home_air_provider[0], atmos_cells), own_target)
    edge_target = one_hot(border_grid_receiver[0], fine_cells) * edge_live[:, None]
    forcing_flat = precise_dot(forcing_atm, own_table)
    edge_table = remap_table(one_hot(border_air_provider[0], atmos_cells), edge_target)
    below_tile = passed_along(forcing_atm, ("mp", "tile"), 1)
    forcing_flat = forcing_flat + precise_dot(below_tile, edge_table)
    driving_input = forcing_flat.reshape(4, tile_y_extent, tile_x_extent)
    drag_damping = (
        jnp.sqrt(driving_input[0] * driving_input[0] + driving_input[1] * driving_input[1] + 0.01)
        / 1.2
    )
    marine_indicator = marine_indicator_grid.astype(jnp.float32)
    marine_variable_bundle = jnp.concatenate([sea_flow_vectors, skin_heat_anomaly[None]], axis=0)
    for _ in range(OSTEPS):
        haloed_lines = padded(marine_variable_bundle, ((("mp", "tile"), 1),), 1)
        marine_variable_bundle = marine_advance(
            marine_variable_bundle,
            haloed_lines,
            driving_input,
            drag_damping,
            subsurface_heat_anomaly,
            marine_indicator,
        )
    tables = spectral_tables(swell_density_table.shape[0], swell_density_table.shape[1])
    swell_power_density = swell_density_table
    for _ in range(WSTEPS):
        haloed_lines = wave_rows(swell_power_density)
        swell_power_density = wave_source(
            advect(swell_power_density, haloed_lines, tables),
            driving_input[2],
            driving_input[3],
            marine_indicator,
            tables,
        )
    roughness = fine_roughness(swell_power_density, drag_damping, tables)
    fine_fields = jnp.stack(
        [
            marine_indicator * roughness,
            marine_indicator * marine_variable_bundle[2],
            marine_indicator,
        ]
    ).reshape(3, -1)
    accumulated_aggregates = lax.dot_general(
        fine_fields,
        own_table,
        (((1,), (1,)), ((), ())),
        precision=lax.Precision.HIGHEST,
        preferred_element_type=jnp.float32,
    )
    edge_sums = lax.dot_general(
        fine_fields,
        edge_table,
        (((1,), (1,)), ((), ())),
        precision=lax.Precision.HIGHEST,
        preferred_element_type=jnp.float32,
    )
    accumulated_aggregates = accumulated_aggregates + passed_along(edge_sums, ("mp", "tile"), -1)
    air_drag_height_tenths = (accumulated_aggregates[0] + 1000.0 * prior_drag_height) / (
        accumulated_aggregates[2] + 1.0
    )
    air_heat_anomaly_back = (accumulated_aggregates[1] + prior_skin_heat_anomaly) / (
        accumulated_aggregates[2] + 1.0
    )
    return (
        marine_variable_bundle[:2],
        marine_variable_bundle[2],
        swell_power_density,
        air_drag_height_tenths,
        air_heat_anomaly_back,
    )


def solution(mesh):
    in_specs = (
        P(None, ("mp", "tile")),
        P(("mp", "tile")),
        P(("mp", "tile")),
        P(None, ("mp", "tile"), None),
        P(("mp", "tile"), None),
        P(("mp", "tile"), None),
        P(None, None, ("mp", "tile"), None),
        P(("mp", "tile"), None),
        P(("mp", "tile"), None),
        P(("mp", "tile"), None),
        P(("mp", "tile"), None),
        P(("mp", "tile"), None),
        P(("mp", "tile"), None),
        P(("mp", "tile"), None),
        P(("mp", "tile"), None),
    )
    out_specs = (
        P(None, ("mp", "tile"), None),
        P(("mp", "tile"), None),
        P(None, None, ("mp", "tile"), None),
        P(("mp", "tile")),
        P(("mp", "tile")),
    )
    return jax.shard_map(
        per_device, mesh=mesh, in_specs=in_specs, out_specs=out_specs, check_vma=False
    )
```

profile of v0, /device:TPU:24, one launch (start us, length us, event | category | flops | bytes accessed | tf_op | source)
XLA Modules:
  0.0 310.2 jit_solution(1531197685390415005)
XLA Ops:
  2.9 4.0 %collective-permute-start = (f32[4,512]{1,0:T(4,128)S(1)}, f32[4,512]{1,0:T(4,128)S(1)}, u32[]{:S(2)}, u32[]{:S(2)}) collective-permute-start(f32[4,512]{1,0:T(4,128)S(1)} %pad_maximum_fusion.38), channel_id=1, source_target_pairs={{0,1},{1,2},{2,3},{3,4},{4,5},{5,6},{6,7},{7,8},{8,9},{9,10},{10,1... | collective-permute-start | bytes 24584 | tf_op jit(solution)/shard_map/ppermute | solution.py:35
  6.8 7.7 %copy.22 = f32[36,32,8,256]{3,1,2,0:T(8,128)S(1)} copy(f32[36,32,8,256]{3,2,1,0:T(8,128)} %param.21) | data formatting | bytes 18874368 | tf_op args[6]
  20.0 6.4 %collective-permute-start.10 = (f32[36,32,1,256]{3,1,2,0:T(8,128)}, f32[36,32,1,256]{3,1,2,0:T(8,128)}, u32[]{:S(2)}, u32[]{:S(2)}) collective-permute-start(f32[36,32,1,256]{3,1,2,0:T(8,128)} %get-tuple-element.37), channel_id=1, source_target_pairs={{1,0},{2,1},{3,2},{4,3},{5,4},{6,5},{7,6},{8,7},{9,8},{10,9},{11,1... | collective-permute-start | bytes 3538952 | tf_op jit(solution)/shard_map/ppermute | solution.py:25
  32.2 37.9 %fusion = f32[512,2048]{1,0:T(8,128)} fusion(f32[4608]{0:T(1024)S(1)} %fusion.79, s32[4608]{0:T(1024)S(1)} %reduce.1, pred[4608,512]{1,0:T(32,128)(4,1)S(1)} %iota_compare_fusion.13), kind=kOutput, calls=%fused_computation | convolution fusion | flops 58000932864 | bytes 6590464 | tf_op jit(solution)/shard_map/dot_general | solution.py:146
  70.1 4.3 %fusion.141 = f32[4,2048]{1,0:T(4,128)S(1)} fusion(f32[512,2048]{1,0:T(8,128)} %fusion, f32[2,512]{1,0:T(2,128)S(1)} %copy-done.9, f32[1,512]{1,0:T(1,128)S(1)} %bitcast.191, f32[1,512]{1,0:T(1,128)S(1)} %bitcast.189), kind=kOutput, calls=%fused_computation.265 | convolution fusion | flops 50335744 | bytes 4235264 | tf_op jit(solution)/shard_map/dot_general | solution.py:142
  75.1 4.1 %fusion.57 = f32[512,2048]{1,0:T(8,128)S(1)} fusion(f32[384]{0:T(512)S(1)} %fusion.131, s32[384]{0:T(512)S(1)} %reduce.4, s32[384]{0:T(512)S(1)} %reduce.3), kind=kOutput, calls=%fused_computation.85 | convolution fusion | flops 4833607680 | bytes 4198912 | tf_op jit(solution)/shard_map/dot_general | solution.py:146
  83.6 17.5 %multiply_reduce_fusion.4 = (f32[8,256]{1,0:T(8,128)S(1)}, f32[36,32,8,256]{3,1,2,0:T(8,128)S(1)}) fusion(f32[32]{0:T(128)S(1)} %get-tuple-element.83, f32[36,32,8,256]{3,1,2,0:T(8,128)} %copy-done, f32[36,32,1,256]{3,1,2,0:T(8,128)} %collective-permute-done.10, f32[36,32]{1,0:T(8,128)S(1)} %get-tuple-element.73, ...), kind=kLoop, calls=%fused_computation.82 | loop fusion | flops 37746688 | bytes 21260416 | tf_op jit(solution)/shard_map/reduce_sum | solution.py:68
  106.1 8.1 %collective-permute-start.12 = (f32[36,32,1,256]{3,1,2,0:T(8,128)S(1)}, f32[36,32,1,256]{3,1,2,0:T(8,128)S(1)}, u32[]{:S(2)}, u32[]{:S(2)}) collective-permute-start(f32[36,32,1,256]{3,1,2,0:T(8,128)S(1)} %get-tuple-element.35), channel_id=1, source_target_pairs={{1,0},{2,1},{3,2},{4,3},{5,4},{6,5},{7,6},{8,7},{9,8},{10,9},{11,1... | collective-permute-start | bytes 3538952 | tf_op jit(solution)/shard_map/ppermute | solution.py:25
  114.3 23.5 %collective-permute-done.11 = f32[36,32,1,256]{3,1,2,0:T(8,128)S(1)} collective-permute-done((f32[36,32,1,256]{3,1,2,0:T(8,128)S(1)}, f32[36,32,1,256]{3,1,2,0:T(8,128)S(1)}, u32[]{:S(2)}, u32[]{:S(2)}) %collective-permute-start.11) | collective-permute-done | bytes 1179680 | tf_op jit(solution)/shard_map/ppermute | solution.py:23
  138.9 9.6 %multiply_reduce_fusion.3 = (f32[8,256]{1,0:T(8,128)S(1)}, f32[36,32,8,256]{3,1,2,0:T(8,128)S(1)}) fusion(f32[32]{0:T(128)S(1)} %get-tuple-element.83, f32[36,32,8,256]{3,1,2,0:T(8,128)S(1)} %multiply_multiply_fusion.3, f32[36,32,1,256]{3,1,2,0:T(8,128)S(1)} %collective-permute-done.12, f32[36,32]{1,0:T(8,128)S(1)} %get-tuple-element.73, ...), kind=kLoop, calls=%fused_computation.80 | loop fusion | flops 37746688 | bytes 21260416 | tf_op jit(solution)/shard_map/reduce_sum | solution.py:68
  153.5 8.6 %collective-permute-start.14 = (f32[36,32,1,256]{3,1,2,0:T(8,128)S(1)}, f32[36,32,1,256]{3,1,2,0:T(8,128)S(1)}, u32[]{:S(2)}, u32[]{:S(2)}) collective-permute-start(f32[36,32,1,256]{3,1,2,0:T(8,128)S(1)} %get-tuple-element.33), channel_id=1, source_target_pairs={{1,0},{2,1},{3,2},{4,3},{5,4},{6,5},{7,6},{8,7},{9,8},{10,9},{11,1... | collective-permute-start | bytes 3538952 | tf_op jit(solution)/shard_map/ppermute | solution.py:25
  162.1 3.9 %collective-permute-start.1 = (f32[3,1,256]{2,1,0:T(1,128)S(1)}, f32[3,1,256]{2,1,0:T(1,128)S(1)}, u32[]{:S(2)}, u32[]{:S(2)}) collective-permute-start(f32[3,1,256]{2,1,0:T(1,128)S(1)} %get-tuple-element.58), channel_id=1, source_target_pairs={{1,0},{2,1},{3,2},{4,3},{5,4},{6,5},{7,6},{8,7},{9,8},{10,9},{11,1... | collective-permute-start | bytes 9224 | tf_op jit(solution)/shard_map/ppermute | solution.py:25
  168.0 16.7 %collective-permute-done.13 = f32[36,32,1,256]{3,1,2,0:T(8,128)S(1)} collective-permute-done((f32[36,32,1,256]{3,1,2,0:T(8,128)S(1)}, f32[36,32,1,256]{3,1,2,0:T(8,128)S(1)}, u32[]{:S(2)}, u32[]{:S(2)}) %collective-permute-start.13) | collective-permute-done | bytes 1179680 | tf_op jit(solution)/shard_map/ppermute | solution.py:23
  185.8 9.4 %multiply_reduce_fusion.2 = (f32[8,256]{1,0:T(8,128)S(1)}, f32[36,32,8,256]{3,1,2,0:T(8,128)S(1)}) fusion(f32[32]{0:T(128)S(1)} %get-tuple-element.83, f32[36,32,8,256]{3,1,2,0:T(8,128)S(1)} %multiply_multiply_fusion.2, f32[36,32,1,256]{3,1,2,0:T(8,128)S(1)} %collective-permute-done.14, f32[36,32]{1,0:T(8,128)S(1)} %get-tuple-element.73, ...), kind=kLoop, calls=%fused_computation.78 | loop fusion | flops 37746688 | bytes 21260416 | tf_op jit(solution)/shard_map/reduce_sum | solution.py:68
  203.8 8.6 %collective-permute-start.16 = (f32[36,32,1,256]{3,1,2,0:T(8,128)S(1)}, f32[36,32,1,256]{3,1,2,0:T(8,128)}, u32[]{:S(2)}, u32[]{:S(2)}) collective-permute-start(f32[36,32,1,256]{3,1,2,0:T(8,128)S(1)} %get-tuple-element.31), channel_id=1, source_target_pairs={{1,0},{2,1},{3,2},{4,3},{5,4},{6,5},{7,6},{8,7},{9,8},{10,9},{11,1... | collective-permute-start | bytes 3538952 | tf_op jit(solution)/shard_map/ppermute | solution.py:25
  212.7 3.9 %collective-permute-start.3 = (f32[3,1,256]{2,1,0:T(1,128)S(1)}, f32[3,1,256]{2,1,0:T(1,128)S(1)}, u32[]{:S(2)}, u32[]{:S(2)}) collective-permute-start(f32[3,1,256]{2,1,0:T(1,128)S(1)} %get-tuple-element.56), channel_id=1, source_target_pairs={{1,0},{2,1},{3,2},{4,3},{5,4},{6,5},{7,6},{8,7},{9,8},{10,9},{11,1... | collective-permute-start | bytes 9224 | tf_op jit(solution)/shard_map/ppermute | solution.py:25
  218.6 16.7 %collective-permute-done.3 = f32[3,1,256]{2,1,0:T(1,128)S(1)} collective-permute-done((f32[3,1,256]{2,1,0:T(1,128)S(1)}, f32[3,1,256]{2,1,0:T(1,128)S(1)}, u32[]{:S(2)}, u32[]{:S(2)}) %collective-permute-start.3) | collective-permute-done | bytes 3104 | tf_op jit(solution)/shard_map/ppermute | solution.py:25
  235.4 17.5 %multiply_reduce_fusion.1 = (f32[8,256]{1,0:T(8,128)S(1)}, f32[36,32,8,256]{3,1,2,0:T(8,128)S(1)}) fusion(f32[32]{0:T(128)S(1)} %get-tuple-element.83, f32[36,32,8,256]{3,1,2,0:T(8,128)} %copy-done.1, f32[36,32,1,256]{3,1,2,0:T(8,128)} %collective-permute-done.16, f32[36,32]{1,0:T(8,128)S(1)} %get-tuple-element.73, ...), kind=kLoop, calls=%fused_computation.76 | loop fusion | flops 37746688 | bytes 21260416 | tf_op jit(solution)/shard_map/reduce_sum | solution.py:68
  256.3 8.7 %collective-permute-start.5 = (f32[3,1,256]{2,1,0:T(1,128)S(1)}, f32[3,1,256]{2,1,0:T(1,128)S(1)}, u32[]{:S(2)}, u32[]{:S(2)}) collective-permute-start(f32[3,1,256]{2,1,0:T(1,128)S(1)} %get-tuple-element.54), channel_id=1, source_target_pairs={{1,0},{2,1},{3,2},{4,3},{5,4},{6,5},{7,6},{8,7},{9,8},{10,9},{11,1... | collective-permute-start | bytes 9224 | tf_op jit(solution)/shard_map/ppermute | solution.py:25
  266.9 7.8 %collective-permute-done.6 = f32[3,1,256]{2,1,0:T(1,128)S(1)} collective-permute-done((f32[3,1,256]{2,1,0:T(1,128)S(1)}, f32[3,1,256]{2,1,0:T(1,128)S(1)}, u32[]{:S(2)}, u32[]{:S(2)}) %collective-permute-start.6) | collective-permute-done | bytes 3104 | tf_op jit(solution)/shard_map/ppermute | solution.py:23
  276.8 4.1 %collective-permute-start.8 = (f32[3,1,256]{2,1,0:T(1,128)S(1)}, f32[3,1,256]{2,1,0:T(1,128)S(1)}, u32[]{:S(2)}, u32[]{:S(2)}) collective-permute-start(f32[3,1,256]{2,1,0:T(1,128)S(1)} %get-tuple-element.53), channel_id=1, source_target_pairs={{0,1},{1,2},{2,3},{3,4},{4,5},{5,6},{6,7},{7,8},{8,9},{9,10},{10,1... | collective-permute-start | bytes 9224 | tf_op jit(solution)/shard_map/ppermute | solution.py:23
  281.0 12.7 %copy.31 = f32[36,32,8,256]{3,2,1,0:T(8,128)} copy(f32[36,32,8,256]{3,1,2,0:T(8,128)S(1)} %get-tuple-element.17) | data formatting | bytes 18874368
  294.4 3.8 %fusion.80 = f32[3,512]{1,0:T(4,128)S(1)} fusion(f32[512,2048]{1,0:T(8,128)S(1)} %copy-done.4, f32[1,2048]{1,0:T(1,128)S(1)} %bitcast.182, f32[1,2048]{1,0:T(1,128)S(1)} %bitcast.186, f32[1,2048]{1,0:T(1,128)S(1)} %bitcast.184), kind=kOutput, calls=%fused_computation.153 | convolution fusion | flops 37761024 | bytes 4225024 | tf_op jit(solution)/shard_map/dot_general | solution.py:243
  298.2 6.1 %collective-permute-start.17 = (f32[3,512]{1,0:T(4,128)S(1)}, f32[3,512]{1,0:T(4,128)S(1)}, u32[]{:S(2)}, u32[]{:S(2)}) collective-permute-start(f32[3,512]{1,0:T(4,128)S(1)} %fusion.80), channel_id=1, source_target_pairs={{1,0},{2,1},{3,2},{4,3},{5,4},{6,5},{7,6},{8,7},{9,8},{10,9},{11,1... | collective-permute-start | bytes 18440 | tf_op jit(solution)/shard_map/ppermute | solution.py:35
  (126 shorter events, 56.9 us)
Async XLA Ops:
  2.9 28.5 %copy-start.12 = (f32[1,4608]{1,0:T(1,128)S(1)}, f32[1,4608]{1,0:T(1,128)}, u32[]{:S(2)}) copy-start(f32[1,4608]{1,0:T(1,128)} %param.25) | copy-start | bytes 55300
  2.9 76.5 %collective-permute-start = (f32[4,512]{1,0:T(4,128)S(1)}, f32[4,512]{1,0:T(4,128)S(1)}, u32[]{:S(2)}, u32[]{:S(2)}) collective-permute-start(f32[4,512]{1,0:T(4,128)S(1)} %pad_maximum_fusion.38), channel_id=1, source_target_pairs={{0,1},{1,2},{2,3},{3,4},{4,5},{5,6},{6,7},{7,8},{8,9},{9,10},{10,1... | collective-permute-start | bytes 24584 | tf_op jit(solution)/shard_map/ppermute | solution.py:35
  20.0 63.6 %collective-permute-start.10 = (f32[36,32,1,256]{3,1,2,0:T(8,128)}, f32[36,32,1,256]{3,1,2,0:T(8,128)}, u32[]{:S(2)}, u32[]{:S(2)}) collective-permute-start(f32[36,32,1,256]{3,1,2,0:T(8,128)} %get-tuple-element.37), channel_id=1, source_target_pairs={{1,0},{2,1},{3,2},{4,3},{5,4},{6,5},{7,6},{8,7},{9,8},{10,9},{11,1... | collective-permute-start | bytes 3538952 | tf_op jit(solution)/shard_map/ppermute | solution.py:25
  26.4 57.2 %collective-permute-start.9 = (f32[36,32,1,256]{3,1,2,0:T(8,128)}, f32[36,32,1,256]{3,1,2,0:T(8,128)}, u32[]{:S(2)}, u32[]{:S(2)}) collective-permute-start(f32[36,32,1,256]{3,1,2,0:T(8,128)} %get-tuple-element.36), channel_id=1, source_target_pairs={{0,1},{1,2},{2,3},{3,4},{4,5},{5,6},{6,7},{7,8},{8,9},{9,10},{10,1... | collective-permute-start | bytes 3538952 | tf_op jit(solution)/shard_map/ppermute | solution.py:23
  32.1 38.0 %copy-start.9 = (f32[2,512]{1,0:T(2,128)S(1)}, f32[2,512]{1,0:T(2,128)}, u32[]{:S(2)}) copy-start(f32[2,512]{1,0:T(2,128)} %param.15) | copy-start | bytes 12292
  32.1 42.2 %copy-start.16 = (f32[1,384]{1,0:T(1,128)S(1)}, f32[1,384]{1,0:T(1,128)}, u32[]{:S(2)}) copy-start(f32[1,384]{1,0:T(1,128)} %param.28) | copy-start | bytes 4612
  32.1 42.3 %copy-start.17 = (s32[1,384]{1,0:T(1,128)S(1)}, s32[1,384]{1,0:T(1,128)}, u32[]{:S(2)}) copy-start(s32[1,384]{1,0:T(1,128)} %param.26) | copy-start | bytes 4612
  32.1 42.3 %copy-start.18 = (s32[1,384]{1,0:T(1,128)S(1)}, s32[1,384]{1,0:T(1,128)}, u32[]{:S(2)}) copy-start(s32[1,384]{1,0:T(1,128)} %param.27) | copy-start | bytes 4612
  32.1 42.3 %copy-start.6 = (s32[8,256]{1,0:T(8,128)S(1)}, s32[8,256]{1,0:T(8,128)}, u32[]{:S(2)}) copy-start(s32[8,256]{1,0:T(8,128)} %param.22) | copy-start | bytes 24580
  104.2 33.5 %collective-permute-start.11 = (f32[36,32,1,256]{3,1,2,0:T(8,128)S(1)}, f32[36,32,1,256]{3,1,2,0:T(8,128)S(1)}, u32[]{:S(2)}, u32[]{:S(2)}) collective-permute-start(f32[36,32,1,256]{3,1,2,0:T(8,128)S(1)} %get-tuple-element.34), channel_id=1, source_target_pairs={{0,1},{1,2},{2,3},{3,4},{4,5},{5,6},{6,7},{7,8},{8,9},{9,10},{10,1... | collective-permute-start | bytes 3538952 | tf_op jit(solution)/shard_map/ppermute | solution.py:23
  106.1 32.8 %collective-permute-start.12 = (f32[36,32,1,256]{3,1,2,0:T(8,128)S(1)}, f32[36,32,1,256]{3,1,2,0:T(8,128)S(1)}, u32[]{:S(2)}, u32[]{:S(2)}) collective-permute-start(f32[36,32,1,256]{3,1,2,0:T(8,128)S(1)} %get-tuple-element.35), channel_id=1, source_target_pairs={{1,0},{2,1},{3,2},{4,3},{5,4},{6,5},{7,6},{8,7},{9,8},{10,9},{11,1... | collective-permute-start | bytes 3538952 | tf_op jit(solution)/shard_map/ppermute | solution.py:25
  151.5 33.1 %collective-permute-start.13 = (f32[36,32,1,256]{3,1,2,0:T(8,128)S(1)}, f32[36,32,1,256]{3,1,2,0:T(8,128)S(1)}, u32[]{:S(2)}, u32[]{:S(2)}) collective-permute-start(f32[36,32,1,256]{3,1,2,0:T(8,128)S(1)} %get-tuple-element.32), channel_id=1, source_target_pairs={{0,1},{1,2},{2,3},{3,4},{4,5},{5,6},{6,7},{7,8},{8,9},{9,10},{10,1... | collective-permute-start | bytes 3538952 | tf_op jit(solution)/shard_map/ppermute | solution.py:23
  153.5 32.4 %collective-permute-start.14 = (f32[36,32,1,256]{3,1,2,0:T(8,128)S(1)}, f32[36,32,1,256]{3,1,2,0:T(8,128)S(1)}, u32[]{:S(2)}, u32[]{:S(2)}) collective-permute-start(f32[36,32,1,256]{3,1,2,0:T(8,128)S(1)} %get-tuple-element.33), channel_id=1, source_target_pairs={{1,0},{2,1},{3,2},{4,3},{5,4},{6,5},{7,6},{8,7},{9,8},{10,9},{11,1... | collective-permute-start | bytes 3538952 | tf_op jit(solution)/shard_map/ppermute | solution.py:25
  162.1 50.3 %collective-permute-start.1 = (f32[3,1,256]{2,1,0:T(1,128)S(1)}, f32[3,1,256]{2,1,0:T(1,128)S(1)}, u32[]{:S(2)}, u32[]{:S(2)}) collective-permute-start(f32[3,1,256]{2,1,0:T(1,128)S(1)} %get-tuple-element.58), channel_id=1, source_target_pairs={{1,0},{2,1},{3,2},{4,3},{5,4},{6,5},{7,6},{8,7},{9,8},{10,9},{11,1... | collective-permute-start | bytes 9224 | tf_op jit(solution)/shard_map/ppermute | solution.py:25
  166.1 46.4 %collective-permute-start.2 = (f32[3,1,256]{2,1,0:T(1,128)S(1)}, f32[3,1,256]{2,1,0:T(1,128)S(1)}, u32[]{:S(2)}, u32[]{:S(2)}) collective-permute-start(f32[3,1,256]{2,1,0:T(1,128)S(1)} %get-tuple-element.59), channel_id=1, source_target_pairs={{0,1},{1,2},{2,3},{3,4},{4,5},{5,6},{6,7},{7,8},{8,9},{9,10},{10,1... | collective-permute-start | bytes 9224 | tf_op jit(solution)/shard_map/ppermute | solution.py:23
  201.9 33.5 %collective-permute-start.15 = (f32[36,32,1,256]{3,1,2,0:T(8,128)S(1)}, f32[36,32,1,256]{3,1,2,0:T(8,128)}, u32[]{:S(2)}, u32[]{:S(2)}) collective-permute-start(f32[36,32,1,256]{3,1,2,0:T(8,128)S(1)} %get-tuple-element.30), channel_id=1, source_target_pairs={{0,1},{1,2},{2,3},{3,4},{4,5},{5,6},{6,7},{7,8},{8,9},{9,10},{10,1... | collective-permute-start | bytes 3538952 | tf_op jit(solution)/shard_map/ppermute | solution.py:23
  203.8 31.5 %collective-permute-start.16 = (f32[36,32,1,256]{3,1,2,0:T(8,128)S(1)}, f32[36,32,1,256]{3,1,2,0:T(8,128)}, u32[]{:S(2)}, u32[]{:S(2)}) collective-permute-start(f32[36,32,1,256]{3,1,2,0:T(8,128)S(1)} %get-tuple-element.31), channel_id=1, source_target_pairs={{1,0},{2,1},{3,2},{4,3},{5,4},{6,5},{7,6},{8,7},{9,8},{10,9},{11,1... | collective-permute-start | bytes 3538952 | tf_op jit(solution)/shard_map/ppermute | solution.py:25
  212.7 22.6 %collective-permute-start.3 = (f32[3,1,256]{2,1,0:T(1,128)S(1)}, f32[3,1,256]{2,1,0:T(1,128)S(1)}, u32[]{:S(2)}, u32[]{:S(2)}) collective-permute-start(f32[3,1,256]{2,1,0:T(1,128)S(1)} %get-tuple-element.56), channel_id=1, source_target_pairs={{1,0},{2,1},{3,2},{4,3},{5,4},{6,5},{7,6},{8,7},{9,8},{10,9},{11,1... | collective-permute-start | bytes 9224 | tf_op jit(solution)/shard_map/ppermute | solution.py:25
  216.6 18.6 %collective-permute-start.4 = (f32[3,1,256]{2,1,0:T(1,128)S(1)}, f32[3,1,256]{2,1,0:T(1,128)S(1)}, u32[]{:S(2)}, u32[]{:S(2)}) collective-permute-start(f32[3,1,256]{2,1,0:T(1,128)S(1)} %get-tuple-element.57), channel_id=1, source_target_pairs={{0,1},{1,2},{2,3},{3,4},{4,5},{5,6},{6,7},{7,8},{8,9},{9,10},{10,1... | collective-permute-start | bytes 9224 | tf_op jit(solution)/shard_map/ppermute | solution.py:23
  256.3 10.6 %collective-permute-start.5 = (f32[3,1,256]{2,1,0:T(1,128)S(1)}, f32[3,1,256]{2,1,0:T(1,128)S(1)}, u32[]{:S(2)}, u32[]{:S(2)}) collective-permute-start(f32[3,1,256]{2,1,0:T(1,128)S(1)} %get-tuple-element.54), channel_id=1, source_target_pairs={{1,0},{2,1},{3,2},{4,3},{5,4},{6,5},{7,6},{8,7},{9,8},{10,9},{11,1... | collective-permute-start | bytes 9224 | tf_op jit(solution)/shard_map/ppermute | solution.py:25
  265.0 9.7 %collective-permute-start.6 = (f32[3,1,256]{2,1,0:T(1,128)S(1)}, f32[3,1,256]{2,1,0:T(1,128)S(1)}, u32[]{:S(2)}, u32[]{:S(2)}) collective-permute-start(f32[3,1,256]{2,1,0:T(1,128)S(1)} %get-tuple-element.55), channel_id=1, source_target_pairs={{0,1},{1,2},{2,3},{3,4},{4,5},{5,6},{6,7},{7,8},{8,9},{9,10},{10,1... | collective-permute-start | bytes 9224 | tf_op jit(solution)/shard_map/ppermute | solution.py:23
  274.8 18.9 %collective-permute-start.7 = (f32[3,1,256]{2,1,0:T(1,128)S(1)}, f32[3,1,256]{2,1,0:T(1,128)S(1)}, u32[]{:S(2)}, u32[]{:S(2)}) collective-permute-start(f32[3,1,256]{2,1,0:T(1,128)S(1)} %get-tuple-element.52), channel_id=1, source_target_pairs={{1,0},{2,1},{3,2},{4,3},{5,4},{6,5},{7,6},{8,7},{9,8},{10,9},{11,1... | collective-permute-start | bytes 9224 | tf_op jit(solution)/shard_map/ppermute | solution.py:25
  276.8 16.9 %collective-permute-start.8 = (f32[3,1,256]{2,1,0:T(1,128)S(1)}, f32[3,1,256]{2,1,0:T(1,128)S(1)}, u32[]{:S(2)}, u32[]{:S(2)}) collective-permute-start(f32[3,1,256]{2,1,0:T(1,128)S(1)} %get-tuple-element.53), channel_id=1, source_target_pairs={{0,1},{1,2},{2,3},{3,4},{4,5},{5,6},{6,7},{7,8},{8,9},{9,10},{10,1... | collective-permute-start | bytes 9224 | tf_op jit(solution)/shard_map/ppermute | solution.py:23
  298.2 7.5 %collective-permute-start.17 = (f32[3,512]{1,0:T(4,128)S(1)}, f32[3,512]{1,0:T(4,128)S(1)}, u32[]{:S(2)}, u32[]{:S(2)}) collective-permute-start(f32[3,512]{1,0:T(4,128)S(1)} %fusion.80), channel_id=1, source_target_pairs={{1,0},{2,1},{3,2},{4,3},{5,4},{6,5},{7,6},{8,7},{9,8},{10,9},{11,1... | collective-permute-start | bytes 18440 | tf_op jit(solution)/shard_map/ppermute | solution.py:35
  (13 other events, 229.4 us)
where the time goes:
time: 316 us; the launch traced here: 310 us
  starting transfers between devices  77.9 us (25%)
  other arithmetic  73.4 us (23%)
  waiting for transfers between devices  67.7 us (21%)
  matrix products  55.8 us (18%)
  local copies, waits for them, and re-layouts  33.7 us (11%)
    reduce_sum x4, other arithmetic, wave_source(): energy_sum = jnp.sum(advected * bin_width, axis=(0, 1))  53.9 us
    ppermute x8, starting transfers between devices, padded(): lax.ppermute(head, axis, [((i + 1) % count, i) for i in range(ends)])  50.2 us
    ppermute x8, waiting for transfers between devices, padded(): lax.ppermute(tail, axis, [(i, (i + 1) % count) for i in range(ends)])  47.9 us
    dot_general x2, matrix products, remap_table(): lax.dot_general(source_hot, target_hot, (((0,), (0,)), ((), ())), precisi...  42 us
    unnamed x43, local copies, waits for them, and re-layouts  29.8 us
    ppermute x8, waiting for transfers between devices, padded(): lax.ppermute(head, axis, [((i + 1) % count, i) for i in range(ends)])  19.1 us
    ppermute x8, starting transfers between devices, padded(): lax.ppermute(tail, axis, [(i, (i + 1) % count) for i in range(ends)])  17.6 us
    ppermute x2, starting transfers between devices, passed_along(): return lax.ppermute(value, axis, pairs)  10.1 us
  transfers between devices with their start and end apart: 18, of which 7 were waited for; matrix products, arithmetic and copies ran while one was open for 29% of the time, Pallas kernels for 0%

commit v1 on v0

v1 whole, which is shorter than its diff:
```python
import functools
import math

import jax
import jax.numpy as jnp
import numpy as np
from jax import lax
from jax.experimental import pallas as pl
from jax.experimental.pallas import tpu as pltpu
from jax.sharding import PartitionSpec as P

MESH = pl.DeviceIdType.MESH
GRAV = 9.81
NDIR = 36
NFREQ = 32
HALF = NDIR // 2
STEPS = 4
LANES = 128
OWN = 4608
EDGE = 384
LIST = OWN + EDGE
CHUNK = 512
GROUP = 3
GROUPS = HALF // GROUP

F32 = jnp.float32
BF16 = jnp.bfloat16

FREQ = 0.04 * 1.1 ** np.arange(NFREQ)
MU = 0.028 / FREQ
INV_SPEED = 2.0 * math.pi * FREQ / GRAV
WIDTH = 0.1 * FREQ * (2.0 * math.pi / NDIR)
ANGLE = (np.arange(NDIR) + 0.5) * (2.0 * math.pi / NDIR)
COS = np.cos(ANGLE)
SIN = np.sin(ANGLE)


def direction_table():
    return np.stack([COS, SIN, np.abs(COS), np.abs(SIN)], axis=1).reshape(-1).astype(np.float32)


def frequency_table():
    rows = np.stack([MU, INV_SPEED, MU * WIDTH, MU / WIDTH])
    return np.broadcast_to(rows[:, :, None], rows.shape + (LANES,)).astype(np.float32)


def iota(shape, dim):
    return lax.broadcasted_iota(jnp.int32, shape, dim)


def spread(row):
    return jnp.broadcast_to(row, (8, row.shape[-1]))


def split_rows(value):
    coarse = value.astype(BF16).astype(F32)
    return jnp.where(iota(value.shape, 0) < 4, coarse, value - coarse)


def main_kernel(
    axis_sizes,
    dirs_in, tally_in, e_in, breeze, drag, heat, flow, skin, subs, marine,
    own_src, own_tgt, own_w, edge_src, edge_tgt, edge_w, freq_in,
    el, eh, cur_out, sst_out, drag_out, heat_out,
    breeze_v, drag_v, heat_v, flow_v, skin_v, subs_v, marine_v,
    osrc_v, otgt_v, ow_v, esrc_v, etgt_v, ew_v, freq,
    bulk_s, bulk_r, flux_s, flux_r, atm_s, atm_r, sea_s, sea_r, frc_s, frc_r, sum_s, sum_r,
    dirs, tally, hot_src, hot_tgt, live_v, field, ocean, state, gather,
    in_sem, e_sem, bulk_ss, bulk_rs, flux_ss, flux_rs, misc_ss, misc_rs,
):
    mp, tile = lax.axis_index("mp"), lax.axis_index("tile")
    n_mp, n_tile = axis_sizes
    count = n_mp * n_tile
    me = mp * n_tile + tile
    up = lax.rem(me + 1, count)
    down = lax.rem(me + count - 1, count)
    up_id = (lax.div(up, n_tile), lax.rem(up, n_tile))
    down_id = (lax.div(down, n_tile), lax.rem(down, n_tile))
    peers = (up_id, down_id)
    has_below = jnp.where(me > 0, 1.0, 0.0).astype(F32)
    has_above = jnp.where(me < count - 1, 1.0, 0.0).astype(F32)
    flags = (has_below, has_above)
    states = (el, eh)

    barrier = pltpu.get_barrier_semaphore()
    for peer in peers:
        pl.semaphore_signal(barrier, inc=1, device_id=peer, device_id_type=MESH)

    small = [
        (breeze, breeze_v), (drag, drag_v), (heat, heat_v), (flow, flow_v), (skin, skin_v),
        (subs, subs_v), (marine, marine_v), (freq_in, freq), (own_src, osrc_v), (own_tgt, otgt_v),
        (own_w, ow_v), (edge_src, esrc_v), (edge_tgt, etgt_v), (edge_w, ew_v),
        (tally_in, tally),
    ]
    small.insert(0, (dirs_in, dirs))
    loads = [pltpu.make_async_copy(s, v, in_sem.at[i]) for i, (s, v) in enumerate(small)]
    for load in loads[:9]:
        load.start()

    def e_load(c, side, half):
        rows = pl.ds(pl.multiple_of((side * HALF + c * GROUP) * 256, 256), GROUP * 256)
        return pltpu.make_async_copy(
            e_in.at[rows, pl.ds(half * LANES, LANES)], states[half].at[rows], e_sem.at[c, side, half]
        )

    for c in range(GROUPS):
        for side in range(2):
            for half in range(2):
                e_load(c, side, half).start()
    for load in loads[9:]:
        load.start()

    def misc(src, dst, index, peer):
        return pltpu.make_async_remote_copy(
            src, dst, misc_ss.at[index], misc_rs.at[index], device_id=peer, device_id_type=MESH
        )

    for load in loads[:3]:
        load.wait()
    wind = breeze_v[...]
    east, north = wind[0:1, :], wind[1:2, :]
    factor = 0.4 / jnp.log(10.0 / drag_v[...])
    factor = factor * factor
    speed = jnp.sqrt(east * east + north * north + 1.0)
    for h in range(4):
        cut = slice(h * LANES, (h + 1) * LANES)
        push = 1.2 * factor[:, cut] * speed[:, cut]
        atm_s[4 * h : 4 * h + 1, :] = push * east[:, cut]
        atm_s[4 * h + 1 : 4 * h + 2, :] = push * north[:, cut]
        atm_s[4 * h + 2 : 4 * h + 3, :] = east[:, cut]
        atm_s[4 * h + 3 : 4 * h + 4, :] = north[:, cut]

    for load in loads[3:9]:
        load.wait()
    ocean_mask = marine_v[...].astype(F32)
    own_fields = [flow_v[0], flow_v[1], skin_v[...], ocean_mask, subs_v[...]]
    for i, value in enumerate(own_fields):
        sea_s[0, 4 * i : 4 * i + 4, :] = value[4:8, :]
        sea_s[1, 4 * i : 4 * i + 4, :] = value[0:4, :]
        ocean[i, 4:12, :] = value

    pl.semaphore_wait(barrier, 2)

    atm_copy = misc(atm_s, atm_r, 0, up_id)
    atm_copy.start()
    sea_copies = [misc(sea_s.at[i], sea_r.at[i], 1 + i, peers[i]) for i in range(2)]
    for copy in sea_copies:
        copy.start()

    def bulk(t, side, c):
        part = pl.ds(c * GROUP, GROUP)
        return pltpu.make_async_remote_copy(
            bulk_s.at[t, side, part], bulk_r.at[t, side, part], bulk_ss.at[t, side],
            bulk_rs.at[t, side], device_id=peers[side], device_id_type=MESH,
        )

    def bulk_all(t, side):
        return pltpu.make_async_remote_copy(
            bulk_s.at[t, side], bulk_r.at[t, side], bulk_ss.at[t, side],
            bulk_rs.at[t, side], device_id=peers[side], device_id_type=MESH,
        )

    def flux(t, side):
        return pltpu.make_async_remote_copy(
            flux_s.at[t, side], flux_r.at[t, side], flux_ss.at[t, side],
            flux_rs.at[t, side], device_id=peers[side], device_id_type=MESH,
        )

    def pack(t, side, kk, totals, neighbour):
        k = side * HALF + kk
        sine = dirs[4 * k + 3]
        coef = 2 if t == 0 else 0
        if neighbour is not None:
            along = [dirs[4 * k] * neighbour[0][h] + dirs[4 * k + 1] * neighbour[1][h] for h in range(2)]
        out = list(totals)
        for g in range(NFREQ // 8):
            weight = freq[coef, 8 * g : 8 * g + 8, :] * sine
            for h in range(2):
                start = k * 256 + 64 * g + (7 if side == 0 else 0)
                rows = states[h][pl.ds(start, 8, stride=8), :]
                bulk_s[t, side, kk, h, 8 * g : 8 * g + 8, :] = rows
                moved = rows * weight
                out[h] = out[h] + moved
                if neighbour is not None:
                    growth = jnp.maximum(along[h] * freq[1, 8 * g : 8 * g + 8, :] - 0.01, 0.0)
                    out[2 + h] = out[2 + h] + moved * growth
        return tuple(out)

    zero = jnp.zeros((8, LANES), F32)

    def send_flux(t, side, totals):
        for i, total in enumerate(totals):
            flux_s[t, side, i] = total
        if len(totals) == 2:
            flux_s[t, side, 2] = zero
            flux_s[t, side, 3] = zero
        flux(t, side).start()

    def first_group(c, carry):
        out = []
        for side in range(2):
            for half in range(2):
                e_load(c, side, half).wait()
            totals = carry[2 * side : 2 * side + 2]
            totals = lax.fori_loop(
                0, GROUP, lambda i, s, side=side: pack(0, side, c * GROUP + i, s, None), totals
            )
            bulk(0, side, c).start()
            out += list(totals)
        return tuple(out)

    fluxes = lax.fori_loop(0, GROUPS, first_group, (zero,) * 4)
    for side in range(2):
        send_flux(0, side, fluxes[2 * side : 2 * side + 2])

    for load in loads[9:]:
        load.wait()

    def to_fine(offset, size, src, tgt, weight, limit, table):
        at = pl.ds(offset, size)
        slot = iota((1, size), 1)
        live = jnp.where(slot < limit, weight, 0.0)
        live_v[:, at] = live
        low = iota((LANES, size), 0)
        hot_s = jnp.where(low == (src & 127), 1.0, 0.0).astype(BF16)
        hot_t = jnp.where(low == (tgt & 127), 1.0, 0.0).astype(BF16)
        hot_src[:, at] = hot_s
        hot_tgt[:, at] = hot_t
        part = jnp.dot(table, hot_s, preferred_element_type=F32)
        part = part[0:16] + part[16:32]
        part = jnp.where((iota((16, size), 0) >> 2) == (src >> 7), part, 0.0)
        part = part[0:8] + part[8:16]
        part = (part + pltpu.roll(part, 4, 0)) * live
        part = split_rows(part)
        high = tgt >> 7
        left = jnp.concatenate([jnp.where(high == h, part, 0.0) for h in range(16)], axis=0)
        return lax.dot_general(
            left.astype(BF16), hot_t, (((1,), (1,)), ((), ())), preferred_element_type=F32
        )

    def two_parts(value):
        coarse = value.astype(BF16).astype(F32)
        return jnp.concatenate([coarse, value - coarse], axis=0).astype(BF16)

    own_table = two_parts(atm_s[...])

    def own_chunk(c, total):
        offset = pl.multiple_of(c * CHUNK, CHUNK)
        at = pl.ds(offset, CHUNK)
        return total + to_fine(
            offset, CHUNK, osrc_v[:, at], otgt_v[:, at], ow_v[:, at], tally[0, 1] - offset, own_table
        )

    total = lax.fori_loop(0, OWN // CHUNK, own_chunk, jnp.zeros((LANES, LANES), F32))
    atm_copy.wait_recv()
    edge_limit = jnp.where(me > 0, tally[0, 0], 0)
    total = total + to_fine(
        OWN, EDGE, esrc_v[...], etgt_v[...], ew_v[...], edge_limit, two_parts(atm_r[...])
    )
    field[...] = total
    forcing = []
    for i in range(4):
        halves = []
        for h in range(2):
            coarse = field[pl.ds(8 * h + i, 8, stride=16), :]
            halves.append(coarse + field[pl.ds(8 * h + i + 4, 8, stride=16), :])
        forcing.append(halves)
        for h in range(2):
            cut = slice(h * LANES, (h + 1) * LANES)
            frc_s[0, 4 * i : 4 * i + 4, cut] = halves[h][4:8, :]
            frc_s[1, 4 * i : 4 * i + 4, cut] = halves[h][0:4, :]
            if i < 2:
                ocean[5 + i, 4:12, cut] = halves[h]
    frc_copies = [misc(frc_s.at[i], frc_r.at[i], 3 + i, peers[i]) for i in range(2)]
    for copy in frc_copies:
        copy.start()

    cuts = [slice(0, LANES), slice(LANES, 2 * LANES)]
    masks = [ocean_mask[:, cut] for cut in cuts]
    friction = [
        jnp.sqrt(forcing[0][h] * forcing[0][h] + forcing[1][h] * forcing[1][h] + 0.01) / 1.2
        for h in range(2)
    ]
    for h in range(2):
        state[0, h] = 0.01 * masks[h] * forcing[2][h]
        state[1, h] = 0.01 * masks[h] * forcing[3][h]

    row8 = iota((8, LANES), 0)
    lane8 = iota((8, LANES), 1)

    def advect(t):
        sums = (zero,) * 4
        for quadrant in range(4):
            west = quadrant in (0, 3)
            south = quadrant < 2

            def one(kk, sums, west=west, south=south, quadrant=quadrant):
                k = quadrant * 9 + kk
                cosine, sine = dirs[4 * k + 2], dirs[4 * k + 3]
                both = cosine + sine
                if west:
                    cos_l = jnp.where(lane8 > 0, cosine, 0.0)
                    cos_h = jnp.full((8, LANES), cosine, F32)
                else:
                    cos_l = jnp.full((8, LANES), cosine, F32)
                    cos_h = jnp.where(lane8 < LANES - 1, cosine, 0.0)
                sin_v = jnp.where(row8 > 0 if south else row8 < 7, sine, 0.0)
                sums = list(sums)
                for m in range(NFREQ):
                    rows = pl.ds(pl.multiple_of(k * 256 + m * 8, 8), 8)
                    e_l, e_h = el[rows, :], eh[rows, :]
                    turn = 1 if west else LANES - 1
                    r_l, r_h = pltpu.roll(e_l, turn, 1), pltpu.roll(e_h, turn, 1)
                    if west:
                        x_l, x_h = r_l, jnp.where(lane8 == 0, r_l, r_h)
                    else:
                        x_l, x_h = jnp.where(lane8 == LANES - 1, r_h, r_l), r_h
                    shift = 1 if south else 7
                    y_l, y_h = pltpu.roll(e_l, shift, 0), pltpu.roll(e_h, shift, 0)
                    scale = float(WIDTH[m]) if t == 0 else 1.0
                    keep = scale - (scale * float(MU[m])) * both
                    gain = scale * float(MU[m])
                    a_l = keep * e_l + gain * (cos_l * x_l + sin_v * y_l)
                    a_h = keep * e_h + gain * (cos_h * x_h + sin_v * y_h)
                    el[rows, :] = a_l
                    eh[rows, :] = a_h
                    p = 2 * (m % 2)
                    sums[p] = sums[p] + a_l
                    sums[p + 1] = sums[p + 1] + a_h
                return tuple(sums)

            sums = lax.fori_loop(0, 9, one, sums)
        return [sums[0] + sums[2], sums[1] + sums[3]]

    def source(t, sums):
        for side in range(2):
            flux(t, side).wait_recv()
        arrived = []
        for side in range(2):
            arrived.append(
                [spread(jnp.sum(flux_r[t, side, i], axis=0, keepdims=True)) * flags[side] for i in range(4)]
            )
        for h in range(2):
            energy = sums[h] + jnp.where(row8 == 0, arrived[0][h], 0.0)
            energy = energy + jnp.where(row8 == 7, arrived[1][h], 0.0)
            kept = masks[h] * (1.0 - 0.3 * energy / (energy + 1.0))
            state[2, h] = kept
            state[3, h] = kept - 0.01 * masks[h]
        return arrived

    def grow(t, neighbours):
        last = t == STEPS - 1

        def group(c, carry):
            out = []
            for side in range(2):
                def one(i, totals, side=side):
                    kk = c * GROUP + i
                    k = side * HALF + kk
                    cosine, sine = dirs[4 * k], dirs[4 * k + 1]
                    along = [cosine * state[0, h] + sine * state[1, h] for h in range(2)]
                    kept = [state[2, h] for h in range(2)]
                    base = [state[3, h] for h in range(2)]
                    totals = list(totals)
                    for m in range(NFREQ):
                        rows = pl.ds(pl.multiple_of(k * 256 + m * 8, 8), 8)
                        for h in range(2):
                            grown = jnp.maximum(along[h] * float(INV_SPEED[m]) + base[h], kept[h])
                            value = states[h][rows, :] * grown
                            if last:
                                p = 2 * (m % 2) + h
                                totals[p] = totals[p] + value
                                value = value * float(1.0 / WIDTH[m])
                            states[h][rows, :] = value
                    if last:
                        return tuple(totals)
                    return pack(t + 1, side, kk, totals, neighbours[side] if neighbours else None)

                if last:
                    carry = lax.fori_loop(0, GROUP, one, carry)
                else:
                    size = len(carry) // 2
                    totals = lax.fori_loop(0, GROUP, one, carry[size * side : size * side + size])
                    bulk(t + 1, side, c).start()
                    out += list(totals)
            return carry if last else tuple(out)

        return lax.fori_loop(0, GROUPS, group, (zero,) * (8 if neighbours else 4))

    def enter(t):
        last = t == STEPS - 1
        coef = 2 if t == 0 else (3 if last else 0)
        for side in range(2):
            bulk_all(t, side).wait_recv()
            edge = 0 if side == 0 else 7
            rows = [[spread(state[i, h, edge : edge + 1, :]) for h in range(2)] for i in range(4)]

            def one(kk, carry, side=side, edge=edge, rows=rows):
                k = side * HALF + kk
                sine = dirs[4 * k + 3] * flags[side]
                along = [dirs[4 * k] * rows[0][h] + dirs[4 * k + 1] * rows[1][h] for h in range(2)]
                for g in range(NFREQ // 8):
                    part = slice(8 * g, 8 * g + 8)
                    weight = freq[coef, part, :] * sine
                    for h in range(2):
                        grown = jnp.maximum(along[h] * freq[1, part, :] + rows[3][h], rows[2][h])
                        at = pl.ds(k * 256 + 64 * g + edge, 8, stride=8)
                        states[h][at, :] = states[h][at, :] + bulk_r[t, side, kk, h, part, :] * weight * grown
                return carry

            lax.fori_loop(0, HALF, one, 0)

    def run_ocean():
        for copy in sea_copies:
            copy.wait_recv()
        for copy in frc_copies:
            copy.wait_recv()
        for side, first in ((0, 0), (1, 12)):
            for i in range(5):
                ocean[i, first : first + 4, :] = sea_r[side, 4 * i : 4 * i + 4, :] * flags[side]
            for i in range(2):
                ocean[5 + i, first : first + 4, :] = frc_r[side, 4 * i : 4 * i + 4, :] * flags[side]
        u, v, q = ocean[0], ocean[1], ocean[2]
        wet, deep, push_u, push_v = ocean[3], ocean[4], ocean[5], ocean[6]
        rub = 0.05 * (jnp.sqrt(push_u * push_u + push_v * push_v + 0.01) / 1.2)
        lane = iota((16, 2 * LANES), 1)

        def lap(w):
            west = jnp.where(lane == 0, 0.0, pltpu.roll(w, 1, 1))
            east = jnp.where(lane == 2 * LANES - 1, 0.0, pltpu.roll(w, 2 * LANES - 1, 1))
            return pltpu.roll(w, 1, 0) + pltpu.roll(w, 15, 0) + west + east - 4.0 * w

        for _ in range(STEPS):
            u, v, q = (
                wet * (u + 0.1 * push_u + 0.2 * v - 0.05 * u + 0.2 * lap(u)),
                wet * (v + 0.1 * push_v - 0.2 * u - 0.05 * v + 0.2 * lap(v)),
                wet * (q + 0.2 * lap(q) - rub * (q - deep)),
            )
        ocean[0], ocean[1], ocean[2] = u, v, q
        cur_out[0] = ocean[0, 4:12, :]
        cur_out[1] = ocean[1, 4:12, :]
        sst_out[...] = ocean[2, 4:12, :]

    for t in range(STEPS):
        sums = advect(t)
        if t == STEPS - 2:
            run_ocean()
        arrived = source(t, sums)
        neighbours = None
        if t == STEPS - 2:
            neighbours = []
            for side, row in ((0, 0), (1, 3)):
                other = 1 - side
                neighbours.append(
                    [
                        [0.01 * spread(frc_r[other, 4 * i + row : 4 * i + row + 1, cut]) for cut in cuts]
                        for i in (2, 3)
                    ]
                )
        fluxes = grow(t, neighbours)
        if t < STEPS - 1:
            size = len(fluxes) // 2
            for side in range(2):
                send_flux(t + 1, side, fluxes[size * side : size * side + size])
            enter(t)

    for h in range(2):
        energy = fluxes[h] + fluxes[2 + h]
        for side, edge in ((0, 0), (1, 7)):
            extra = state[2, h] * arrived[side][h] + masks[h] * arrived[side][2 + h]
            energy = energy + jnp.where(row8 == edge, extra, 0.0)
        height = 4.0 * jnp.sqrt(energy + 1e-6)
        rough = 1000.0 * ((0.011 + 0.02 * height) * friction[h] / GRAV + 1.5e-5)
        values = [masks[h] * rough, masks[h] * ocean[2, 4:12, cuts[h]], masks[h], zero]
        for i, value in enumerate(values):
            coarse = value.astype(BF16).astype(F32)
            gather[pl.ds(8 * h + i, 8, stride=16), :] = coarse
            gather[pl.ds(8 * h + i + 4, 8, stride=16), :] = value - coarse
    table = gather[...].astype(BF16)

    def to_coarse(at, size, src, tgt):
        part = jnp.dot(table, hot_tgt[:, at], preferred_element_type=F32)
        high = tgt >> 7
        value = jnp.zeros((8, size), F32)
        for h in range(16):
            value = value + jnp.where(high == h, part[8 * h : 8 * h + 8], 0.0)
        value = (value + pltpu.roll(value, 4, 0)) * live_v[:, at]
        value = split_rows(value)
        left = jnp.concatenate([jnp.where((src >> 7) == h, value, 0.0) for h in range(4)], axis=0)
        return lax.dot_general(
            left.astype(BF16), hot_src[:, at], (((1,), (1,)), ((), ())), preferred_element_type=F32
        )

    def joined(value):
        return jnp.concatenate(
            [value[8 * h : 8 * h + 4] + value[8 * h + 4 : 8 * h + 8] for h in range(4)], axis=0
        )

    sum_s[...] = joined(to_coarse(pl.ds(OWN, EDGE), EDGE, esrc_v[...], etgt_v[...]))
    sum_copy = misc(sum_s, sum_r, 5, down_id)
    sum_copy.start()

    def back_chunk(c, total):
        at = pl.ds(pl.multiple_of(c * CHUNK, CHUNK), CHUNK)
        return total + to_coarse(at, CHUNK, osrc_v[:, at], otgt_v[:, at])

    own_sums = joined(lax.fori_loop(0, OWN // CHUNK, back_chunk, jnp.zeros((32, LANES), F32)))

    enter(STEPS - 1)

    sum_copy.wait_recv()
    totals = own_sums + sum_r[...] * has_above
    for h in range(4):
        cut = slice(h * LANES, (h + 1) * LANES)
        share = totals[4 * h + 2 : 4 * h + 3] + 1.0
        drag_out[:, cut] = (totals[4 * h : 4 * h + 1] + 1000.0 * drag_v[:, cut]) / share
        heat_out[:, cut] = (totals[4 * h + 1 : 4 * h + 2] + heat_v[:, cut]) / share

    for copy in [atm_copy, sum_copy] + sea_copies + frc_copies:
        copy.wait_send()
    for t in range(STEPS):
        for side in range(2):
            bulk_all(t, side).wait_send()
            flux(t, side).wait_send()


def write_kernel(el, eh, cur, sst, drag, heat, e_out, cur_out, sst_out, drag_out, heat_out, sems):
    parts = 9
    size = el.shape[0] // parts
    copies = []
    for c in range(parts):
        rows = pl.ds(c * size, size)
        for h, ref in enumerate((el, eh)):
            copies.append((ref.at[rows], e_out.at[rows, pl.ds(h * LANES, LANES)]))
    copies += [(cur, cur_out), (sst, sst_out), (drag, drag_out), (heat, heat_out)]
    copies = [pltpu.make_async_copy(s, d, sems.at[i]) for i, (s, d) in enumerate(copies)]
    for copy in copies:
        copy.start()
    for copy in copies:
        copy.wait()


def per_device(
    axis_sizes, breeze, drag, heat, flow, skin, subs, swell, marine, own_src, own_tgt, own_w,
    edge_src, edge_tgt, edge_w, tally,
):
    ndir, nfreq, rows, columns = swell.shape
    cells = drag.shape[0]
    lines = ndir * nfreq * rows
    swell = swell.reshape(lines, columns)
    hbm_spec = pl.BlockSpec(memory_space=pltpu.HBM)
    vmem_spec = pl.BlockSpec(memory_space=pltpu.VMEM)
    small_out = [((2, rows, columns), F32), ((rows, columns), F32), ((1, cells), F32), ((1, cells), F32)]
    vmem = pltpu.VMEM
    dma = pltpu.SemaphoreType.DMA
    results = pl.pallas_call(
        functools.partial(main_kernel, axis_sizes),
        out_shape=[vmem((lines, LANES), F32)] * 2 + [vmem(s, d) for s, d in small_out],
        in_specs=[hbm_spec] * 17,
        out_specs=[vmem_spec] * 6,
        scratch_shapes=[
            vmem(breeze.shape, F32), vmem((1, cells), F32), vmem((1, cells), F32), vmem(flow.shape, F32),
            vmem(skin.shape, F32), vmem(subs.shape, F32), vmem(marine.shape, jnp.int32),
            vmem((1, OWN), jnp.int32), vmem((1, OWN), jnp.int32), vmem((1, OWN), F32),
            vmem((1, EDGE), jnp.int32), vmem((1, EDGE), jnp.int32), vmem((1, EDGE), F32),
            vmem((4, NFREQ, LANES), F32),
            vmem((STEPS, 2, HALF, 2, NFREQ, LANES), F32),
            vmem((STEPS, 2, HALF, 2, NFREQ, LANES), F32),
            vmem((STEPS, 2, 4, 8, LANES), F32), vmem((STEPS, 2, 4, 8, LANES), F32),
            vmem((16, LANES), F32), vmem((16, LANES), F32),
            vmem((2, 20, columns), F32), vmem((2, 20, columns), F32),
            vmem((2, 16, columns), F32), vmem((2, 16, columns), F32),
            vmem((16, LANES), F32), vmem((16, LANES), F32),
            pltpu.SMEM((4 * NDIR,), F32), pltpu.SMEM((1, 2), jnp.int32),
            vmem((LANES, LIST), BF16), vmem((LANES, LIST), BF16), vmem((1, LIST), F32),
            vmem((LANES, LANES), F32), vmem((7, 16, columns), F32), vmem((4, 2, 8, LANES), F32),
            vmem((LANES, LANES), F32),
            dma((16,)), dma((GROUPS, 2, 2)),
            dma((STEPS, 2)), dma((STEPS, 2)), dma((STEPS, 2)), dma((STEPS, 2)), dma((6,)), dma((6,)),
        ],
        compiler_params=pltpu.CompilerParams(
            collective_id=0, has_side_effects=True, vmem_limit_bytes=36 * 2**20
        ),
        name="coupled_step",
    )(*(pltpu.with_memory_space_constraint(x, pltpu.HBM) for x in (
        jnp.asarray(direction_table()), tally, swell, breeze, drag.reshape(1, cells), heat.reshape(1, cells),
        flow, skin, subs, marine, own_src, own_tgt, own_w, edge_src, edge_tgt, edge_w,
        jnp.asarray(frequency_table()),
    )))
    outs = pl.pallas_call(
        write_kernel,
        out_shape=[jax.ShapeDtypeStruct((lines, columns), F32)]
        + [jax.ShapeDtypeStruct(s, d) for s, d in small_out],
        in_specs=[vmem_spec] * 6,
        out_specs=[hbm_spec] * 5,
        scratch_shapes=[dma((22,))],
        name="write_out",
    )(*results)
    spectrum, currents, sst, drag_out, heat_out = outs
    return (
        currents,
        sst,
        spectrum.reshape(ndir, nfreq, rows, columns),
        drag_out.reshape(cells),
        heat_out.reshape(cells),
    )


def solution(mesh):
    both = ("mp", "tile")
    flat, grid, pair = P(both), P(both, None), P(None, both, None)
    in_specs = (P(None, both), flat, flat, pair, grid, grid, P(None, None, both, None)) + (grid,) * 8
    out_specs = (pair, grid, P(None, None, both, None), flat, flat)
    sizes = (mesh.shape["mp"], mesh.shape["tile"])
    return jax.shard_map(
        functools.partial(per_device, sizes), mesh=mesh, in_specs=in_specs, out_specs=out_specs, check_vma=False
    )
```

time: 316 us -> 103 us (0.33)
  the two profiles are of different devices: /device:TPU:24 before, /device:TPU:1 now
where the time goes in v1:
time: 103 us
  Pallas kernels  95.5 us (93%)
  local copies, waits for them, and re-layouts  6.67 us (6%)
    pallas_call x1, Pallas kernels, per_device(): pl.pallas_call(functools.partial(main_kernel, axis_sizes), out_shape=[vme...  87.9 us
    pallas_call x1, Pallas kernels, per_device(): pl.pallas_call(write_kernel, out_shape=[jax.ShapeDtypeStruct((lines, colu...  7.59 us
    unnamed x12, local copies, waits for them, and re-layouts  6.67 us

profile of v1, /device:TPU:1, one launch (start us, length us, event | category | flops | bytes accessed | tf_op | source)
XLA Modules:
  0.0 102.8 jit_solution(17987430482603553059)
XLA Ops:
  0.6 87.9 %coupled_step.1 = (f32[9216,128]{1,0:T(8,128)S(1)}, f32[9216,128]{1,0:T(8,128)S(1)}, f32[2,8,256]{2,1,0:T(8,128)S(1)}, f32[8,256]{1,0:T(8,128)S(1)}, f32[1,512]{1,0:T(1,128)S(1)}, /*index=5*/f32[1,512]{1,0:T(1,128)S(1)}) custom-call(f32[144]{0:T(256)} %constant.4.clone.dirs_in, s32[1,2]{1,0:T(1,128)} %tally_in.1, f32[9216,256]{1,0:T(8,128)} %bitcast.6, ...), custom_call_target="tpu_custom_call" | custom-call | tf_op jit(solution)/shard_map/coupled_step/pallas_call | solution.py:556
  88.5 0.0 copy-start
  88.6 2.1 %copy-done = f32[9216,128]{1,0:T(8,128)} copy-done((f32[9216,128]{1,0:T(8,128)}, f32[9216,128]{1,0:T(8,128)S(1)}, u32[]{:S(2)}) %copy-start) | copy-done | bytes 4718616
  90.7 0.0 copy-start.1
  90.7 2.2 %copy-done.1 = f32[9216,128]{1,0:T(8,128)} copy-done((f32[9216,128]{1,0:T(8,128)}, f32[9216,128]{1,0:T(8,128)S(1)}, u32[]{:S(2)}) %copy-start.1) | copy-done | bytes 4718616
  92.8 0.0 copy-start.2
  92.9 0.6 copy-done.2
  93.4 0.0 copy-start.3
  93.4 0.6 copy-done.3
  94.0 0.0 copy-start.4
  94.0 0.6 copy-done.4
  94.6 0.0 copy-start.5
  94.6 0.6 copy-done.5
  95.2 7.6 %write_out.1 = (f32[9216,256]{1,0:T(8,128)}, f32[2,8,256]{2,1,0:T(8,128)}, f32[8,256]{1,0:T(8,128)}, f32[1,512]{1,0:T(1,128)}, f32[1,512]{1,0:T(1,128)}) custom-call(f32[9216,128]{1,0:T(8,128)} %copy-done, f32[9216,128]{1,0:T(8,128)} %copy-done.1, f32[2,8,256]{2,1,0:T(8,128)} %copy-done.2, f32[8,256]{1,0:T(8,128)} %copy-done.3, f32[1,512]{1,0:T(1,128)} %copy-done.4, ...), custom_call_target="tpu_custom_call" | custom-call | tf_op jit(solution)/shard_map/write_out/pallas_call | solution.py:590
Async XLA Ops:
  88.5 2.1 %copy-start = (f32[9216,128]{1,0:T(8,128)}, f32[9216,128]{1,0:T(8,128)S(1)}, u32[]{:S(2)}) copy-start(f32[9216,128]{1,0:T(8,128)S(1)} %get-tuple-element.16.el) | copy-start | bytes 14155780
  90.7 2.2 %copy-start.1 = (f32[9216,128]{1,0:T(8,128)}, f32[9216,128]{1,0:T(8,128)S(1)}, u32[]{:S(2)}) copy-start(f32[9216,128]{1,0:T(8,128)S(1)} %get-tuple-element.17.eh) | copy-start | bytes 14155780
  92.8 0.6 copy-start.2
  93.4 0.6 copy-start.3
  94.0 0.6 copy-start.4
  94.6 0.6 copy-start.5

commit v2 on v1

--- a/solution.py
+++ b/solution.py
@@ -22,6 +22,7 @@
 CHUNK = 512
 GROUP = 3
 GROUPS = HALF // GROUP
+EARLY = 3
 
 F32 = jnp.float32
 BF16 = jnp.bfloat16
@@ -77,14 +78,15 @@
     up_id = (lax.div(up, n_tile), lax.rem(up, n_tile))
     down_id = (lax.div(down, n_tile), lax.rem(down, n_tile))
     peers = (up_id, down_id)
-    has_below = jnp.where(me > 0, 1.0, 0.0).astype(F32)
-    has_above = jnp.where(me < count - 1, 1.0, 0.0).astype(F32)
-    flags = (has_below, has_above)
+    sends = (me < count - 1, me > 0)
+    receives = (me > 0, me < count - 1)
     states = (el, eh)
 
     barrier = pltpu.get_barrier_semaphore()
-    for peer in peers:
-        pl.semaphore_signal(barrier, inc=1, device_id=peer, device_id_type=MESH)
+    for side in range(2):
+        @pl.when(sends[side])
+        def _(side=side):
+            pl.semaphore_signal(barrier, inc=1, device_id=peers[side], device_id_type=MESH)
 
     small = [
         (breeze, breeze_v), (drag, drag_v), (heat, heat_v), (flow, flow_v), (skin, skin_v),
@@ -139,13 +141,24 @@
         sea_s[1, 4 * i : 4 * i + 4, :] = value[0:4, :]
         ocean[i, 4:12, :] = value
 
-    pl.semaphore_wait(barrier, 2)
+    for side in range(2):
+        @pl.when(jnp.logical_not(receives[side]))
+        def _(side=side):
+            sea_r[side] = jnp.zeros(sea_r.shape[1:], F32)
+            frc_r[side] = jnp.zeros(frc_r.shape[1:], F32)
+            for t in range(STEPS):
+                flux_r[t, side] = jnp.zeros(flux_r.shape[2:], F32)
+            lone = atm_r if side == 0 else sum_r
+            lone[...] = jnp.zeros(lone.shape, F32)
+
+    inner = (me > 0) & (me < count - 1)
+    pl.semaphore_wait(barrier, jnp.where(inner, 2, 1).astype(jnp.int32))
 
     atm_copy = misc(atm_s, atm_r, 0, up_id)
-    atm_copy.start()
+    pl.when(sends[0])(atm_copy.start)
     sea_copies = [misc(sea_s.at[i], sea_r.at[i], 1 + i, peers[i]) for i in range(2)]
-    for copy in sea_copies:
-        copy.start()
+    for side in range(2):
+        pl.when(sends[side])(sea_copies[side].start)
 
     def bulk(t, side, c):
         part = pl.ds(c * GROUP, GROUP)
@@ -194,7 +207,7 @@
         if len(totals) == 2:
             flux_s[t, side, 2] = zero
             flux_s[t, side, 3] = zero
-        flux(t, side).start()
+        pl.when(sends[side])(flux(t, side).start)
 
     def first_group(c, carry):
         out = []
@@ -205,13 +218,16 @@
             totals = lax.fori_loop(
                 0, GROUP, lambda i, s, side=side: pack(0, side, c * GROUP + i, s, None), totals
             )
-            bulk(0, side, c).start()
+            pl.when(sends[side] & (c < EARLY))(bulk(0, side, c).start)
             out += list(totals)
         return tuple(out)
 
     fluxes = lax.fori_loop(0, GROUPS, first_group, (zero,) * 4)
     for side in range(2):
         send_flux(0, side, fluxes[2 * side : 2 * side + 2])
+    for c in range(EARLY, GROUPS):
+        for side in range(2):
+            pl.when(sends[side])(bulk(0, side, c).start)
 
     for load in loads[9:]:
         load.wait()
@@ -252,7 +268,7 @@
         )
 
     total = lax.fori_loop(0, OWN // CHUNK, own_chunk, jnp.zeros((LANES, LANES), F32))
-    atm_copy.wait_recv()
+    pl.when(receives[0])(atm_copy.wait_recv)
     edge_limit = jnp.where(me > 0, tally[0, 0], 0)
     total = total + to_fine(
         OWN, EDGE, esrc_v[...], etgt_v[...], ew_v[...], edge_limit, two_parts(atm_r[...])
@@ -272,8 +288,8 @@
             if i < 2:
                 ocean[5 + i, 4:12, cut] = halves[h]
     frc_copies = [misc(frc_s.at[i], frc_r.at[i], 3 + i, peers[i]) for i in range(2)]
-    for copy in frc_copies:
-        copy.start()
+    for side in range(2):
+        pl.when(sends[side])(frc_copies[side].start)
 
     cuts = [slice(0, LANES), slice(LANES, 2 * LANES)]
     masks = [ocean_mask[:, cut] for cut in cuts]
@@ -334,11 +350,11 @@
 
     def source(t, sums):
         for side in range(2):
-            flux(t, side).wait_recv()
+            pl.when(receives[side])(flux(t, side).wait_recv)
         arrived = []
         for side in range(2):
             arrived.append(
-                [spread(jnp.sum(flux_r[t, side, i], axis=0, keepdims=True)) * flags[side] for i in range(4)]
+                [spread(jnp.sum(flux_r[t, side, i], axis=0, keepdims=True)) for i in range(4)]
             )
         for h in range(2):
             energy = sums[h] + jnp.where(row8 == 0, arrived[0][h], 0.0)
@@ -381,7 +397,6 @@
                 else:
                     size = len(carry) // 2
                     totals = lax.fori_loop(0, GROUP, one, carry[size * side : size * side + size])
-                    bulk(t + 1, side, c).start()
                     out += list(totals)
             return carry if last else tuple(out)
 
@@ -391,13 +406,11 @@
         last = t == STEPS - 1
         coef = 2 if t == 0 else (3 if last else 0)
         for side in range(2):
-            bulk_all(t, side).wait_recv()
             edge = 0 if side == 0 else 7
-            rows = [[spread(state[i, h, edge : edge + 1, :]) for h in range(2)] for i in range(4)]
-
-            def one(kk, carry, side=side, edge=edge, rows=rows):
+            def one(kk, carry, side=side, edge=edge):
                 k = side * HALF + kk
-                sine = dirs[4 * k + 3] * flags[side]
+                sine = dirs[4 * k + 3]
+                rows = [[spread(state[i, h, edge : edge + 1, :]) for h in range(2)] for i in range(4)]
                 along = [dirs[4 * k] * rows[0][h] + dirs[4 * k + 1] * rows[1][h] for h in range(2)]
                 for g in range(NFREQ // 8):
                     part = slice(8 * g, 8 * g + 8)
@@ -408,18 +421,20 @@
                         states[h][at, :] = states[h][at, :] + bulk_r[t, side, kk, h, part, :] * weight * grown
                 return carry
 
-            lax.fori_loop(0, HALF, one, 0)
+            @pl.when(receives[side])
+            def _():
+                bulk_all(t, side).wait_recv()
+                lax.fori_loop(0, HALF, one, 0)
 
     def run_ocean():
-        for copy in sea_copies:
-            copy.wait_recv()
-        for copy in frc_copies:
-            copy.wait_recv()
+        for side in range(2):
+            pl.when(receives[side])(sea_copies[side].wait_recv)
+            pl.when(receives[side])(frc_copies[side].wait_recv)
         for side, first in ((0, 0), (1, 12)):
             for i in range(5):
-                ocean[i, first : first + 4, :] = sea_r[side, 4 * i : 4 * i + 4, :] * flags[side]
+                ocean[i, first : first + 4, :] = sea_r[side, 4 * i : 4 * i + 4, :]
             for i in range(2):
-                ocean[5 + i, first : first + 4, :] = frc_r[side, 4 * i : 4 * i + 4, :] * flags[side]
+                ocean[5 + i, first : first + 4, :] = frc_r[side, 4 * i : 4 * i + 4, :]
         u, v, q = ocean[0], ocean[1], ocean[2]
         wet, deep, push_u, push_v = ocean[3], ocean[4], ocean[5], ocean[6]
         rub = 0.05 * (jnp.sqrt(push_u * push_u + push_v * push_v + 0.01) / 1.2)
@@ -462,6 +477,8 @@
             size = len(fluxes) // 2
             for side in range(2):
                 send_flux(t + 1, side, fluxes[size * side : size * side + size])
+            for side in range(2):
+                pl.when(sends[side])(bulk_all(t + 1, side).start)
             enter(t)
 
     for h in range(2):
@@ -498,7 +515,7 @@
 
     sum_s[...] = joined(to_coarse(pl.ds(OWN, EDGE), EDGE, esrc_v[...], etgt_v[...]))
     sum_copy = misc(sum_s, sum_r, 5, down_id)
-    sum_copy.start()
+    pl.when(sends[1])(sum_copy.start)
 
     def back_chunk(c, total):
         at = pl.ds(pl.multiple_of(c * CHUNK, CHUNK), CHUNK)
@@ -508,20 +525,22 @@
 
     enter(STEPS - 1)
 
-    sum_copy.wait_recv()
-    totals = own_sums + sum_r[...] * has_above
+    pl.when(receives[1])(sum_copy.wait_recv)
+    totals = own_sums + sum_r[...]
     for h in range(4):
         cut = slice(h * LANES, (h + 1) * LANES)
         share = totals[4 * h + 2 : 4 * h + 3] + 1.0
         drag_out[:, cut] = (totals[4 * h : 4 * h + 1] + 1000.0 * drag_v[:, cut]) / share
         heat_out[:, cut] = (totals[4 * h + 1 : 4 * h + 2] + heat_v[:, cut]) / share
 
-    for copy in [atm_copy, sum_copy] + sea_copies + frc_copies:
-        copy.wait_send()
-    for t in range(STEPS):
-        for side in range(2):
-            bulk_all(t, side).wait_send()
-            flux(t, side).wait_send()
+    for side in range(2):
+        @pl.when(sends[side])
+        def _(side=side):
+            for copy in ((atm_copy, sum_copy)[side], sea_copies[side], frc_copies[side]):
+                copy.wait_send()
+            for t in range(STEPS):
+                bulk_all(t, side).wait_send()
+                flux(t, side).wait_send()
 
 
 def write_kernel(el, eh, cur, sst, drag, heat, e_out, cur_out, sst_out, drag_out, heat_out, sems):
@@ -594,8 +613,9 @@
         in_specs=[vmem_spec] * 6,
         out_specs=[hbm_spec] * 5,
         scratch_shapes=[dma((22,))],
+        compiler_params=pltpu.CompilerParams(vmem_limit_bytes=4 * 2**20),
         name="write_out",
-    )(*results)
+    )(*(pltpu.with_memory_space_constraint(x, pltpu.VMEM) for x in results))
     spectrum, currents, sst, drag_out, heat_out = outs
     return (
         currents,

time: 103 us -> 69.1 us (0.67)
  the two profiles are of different devices: /device:TPU:1 before, /device:TPU:24 now
where the time goes in v2:
time: 69.1 us; the launch traced here: 69 us
  Pallas kernels  68.3 us (99%)
    pallas_call x1, Pallas kernels, per_device(): pl.pallas_call(functools.partial(main_kernel, axis_sizes), out_shape=[vme...  64.5 us
    pallas_call x1, Pallas kernels, per_device(): pl.pallas_call(write_kernel, out_shape=[jax.ShapeDtypeStruct((lines, colu...  3.79 us

profile of v2, /device:TPU:24, one launch (start us, length us, event | category | flops | bytes accessed | tf_op | source)
XLA Modules:
  0.0 69.0 jit_solution(11175485308283845908)
XLA Ops:
  0.6 64.5 %coupled_step.1 = (f32[9216,128]{1,0:T(8,128)S(1)}, f32[9216,128]{1,0:T(8,128)S(1)}, f32[2,8,256]{2,1,0:T(8,128)S(1)}, f32[8,256]{1,0:T(8,128)S(1)}, f32[1,512]{1,0:T(1,128)S(1)}, /*index=5*/f32[1,512]{1,0:T(1,128)S(1)}) custom-call(f32[144]{0:T(256)} %constant.4.clone.dirs_in, s32[1,2]{1,0:T(1,128)} %tally_in.1, f32[9216,256]{1,0:T(8,128)} %bitcast.6, ...), custom_call_target="tpu_custom_call" | custom-call | tf_op jit(solution)/shard_map/coupled_step/pallas_call | solution.py:575
  65.2 3.8 %write_out.1 = (f32[9216,256]{1,0:T(8,128)}, f32[2,8,256]{2,1,0:T(8,128)}, f32[8,256]{1,0:T(8,128)}, f32[1,512]{1,0:T(1,128)}, f32[1,512]{1,0:T(1,128)}) custom-call(f32[9216,128]{1,0:T(8,128)S(1)} %get-tuple-element.16.el, f32[9216,128]{1,0:T(8,128)S(1)} %get-tuple-element.17.eh, f32[2,8,256]{2,1,0:T(8,128)S(1)} %get-tuple-element.18.cur, ...), custom_call_target="tpu_custom_call" | custom-call | tf_op jit(solution)/shard_map/write_out/pallas_call | solution.py:609

commit v3 on v2

--- a/solution.py
+++ b/solution.py
@@ -20,9 +20,9 @@
 EDGE = 384
 LIST = OWN + EDGE
 CHUNK = 512
-GROUP = 3
-GROUPS = HALF // GROUP
-EARLY = 3
+AHEAD = 6
+PART = 3
+EARLY = 9
 
 F32 = jnp.float32
 BF16 = jnp.bfloat16
@@ -67,7 +67,7 @@
     osrc_v, otgt_v, ow_v, esrc_v, etgt_v, ew_v, freq,
     bulk_s, bulk_r, flux_s, flux_r, atm_s, atm_r, sea_s, sea_r, frc_s, frc_r, sum_s, sum_r,
     dirs, tally, hot_src, hot_tgt, live_v, field, ocean, state, gather,
-    in_sem, e_sem, bulk_ss, bulk_rs, flux_ss, flux_rs, misc_ss, misc_rs,
+    in_sem, e_sem, bulk_ss, bulk_rs, last_ss, last_rs, flux_ss, flux_rs, misc_ss, misc_rs,
 ):
     mp, tile = lax.axis_index("mp"), lax.axis_index("tile")
     n_mp, n_tile = axis_sizes
@@ -90,25 +90,28 @@
 
     small = [
         (breeze, breeze_v), (drag, drag_v), (heat, heat_v), (flow, flow_v), (skin, skin_v),
-        (subs, subs_v), (marine, marine_v), (freq_in, freq), (own_src, osrc_v), (own_tgt, otgt_v),
+        (subs, subs_v), (marine, marine_v), (own_src, osrc_v), (own_tgt, otgt_v),
         (own_w, ow_v), (edge_src, esrc_v), (edge_tgt, etgt_v), (edge_w, ew_v),
         (tally_in, tally),
     ]
-    small.insert(0, (dirs_in, dirs))
+    small = [(dirs_in, dirs), (freq_in, freq)] + small
     loads = [pltpu.make_async_copy(s, v, in_sem.at[i]) for i, (s, v) in enumerate(small)]
     for load in loads[:9]:
         load.start()
 
-    def e_load(c, side, half):
-        rows = pl.ds(pl.multiple_of((side * HALF + c * GROUP) * 256, 256), GROUP * 256)
+    def e_load(kk, side, half):
+        rows = pl.ds(pl.multiple_of((side * HALF + kk) * 256, 256), 256)
         return pltpu.make_async_copy(
-            e_in.at[rows, pl.ds(half * LANES, LANES)], states[half].at[rows], e_sem.at[c, side, half]
-        )
-
-    for c in range(GROUPS):
+            e_in.at[rows, pl.ds(half * LANES, LANES)], states[half].at[rows], e_sem.at[kk, side, half]
+        )
+
+    def e_start(kk):
         for side in range(2):
             for half in range(2):
-                e_load(c, side, half).start()
+                e_load(kk, side, half).start()
+
+    for kk in range(AHEAD):
+        e_start(kk)
     for load in loads[9:]:
         load.start()
 
@@ -116,30 +119,6 @@
         return pltpu.make_async_remote_copy(
             src, dst, misc_ss.at[index], misc_rs.at[index], device_id=peer, device_id_type=MESH
         )
-
-    for load in loads[:3]:
-        load.wait()
-    wind = breeze_v[...]
-    east, north = wind[0:1, :], wind[1:2, :]
-    factor = 0.4 / jnp.log(10.0 / drag_v[...])
-    factor = factor * factor
-    speed = jnp.sqrt(east * east + north * north + 1.0)
-    for h in range(4):
-        cut = slice(h * LANES, (h + 1) * LANES)
-        push = 1.2 * factor[:, cut] * speed[:, cut]
-        atm_s[4 * h : 4 * h + 1, :] = push * east[:, cut]
-        atm_s[4 * h + 1 : 4 * h + 2, :] = push * north[:, cut]
-        atm_s[4 * h + 2 : 4 * h + 3, :] = east[:, cut]
-        atm_s[4 * h + 3 : 4 * h + 4, :] = north[:, cut]
-
-    for load in loads[3:9]:
-        load.wait()
-    ocean_mask = marine_v[...].astype(F32)
-    own_fields = [flow_v[0], flow_v[1], skin_v[...], ocean_mask, subs_v[...]]
-    for i, value in enumerate(own_fields):
-        sea_s[0, 4 * i : 4 * i + 4, :] = value[4:8, :]
-        sea_s[1, 4 * i : 4 * i + 4, :] = value[0:4, :]
-        ocean[i, 4:12, :] = value
 
     for side in range(2):
         @pl.when(jnp.logical_not(receives[side]))
@@ -154,16 +133,9 @@
     inner = (me > 0) & (me < count - 1)
     pl.semaphore_wait(barrier, jnp.where(inner, 2, 1).astype(jnp.int32))
 
-    atm_copy = misc(atm_s, atm_r, 0, up_id)
-    pl.when(sends[0])(atm_copy.start)
-    sea_copies = [misc(sea_s.at[i], sea_r.at[i], 1 + i, peers[i]) for i in range(2)]
-    for side in range(2):
-        pl.when(sends[side])(sea_copies[side].start)
-
-    def bulk(t, side, c):
-        part = pl.ds(c * GROUP, GROUP)
+    def bulk(t, side, kk):
         return pltpu.make_async_remote_copy(
-            bulk_s.at[t, side, part], bulk_r.at[t, side, part], bulk_ss.at[t, side],
+            bulk_s.at[t, side, kk], bulk_r.at[t, side, kk], bulk_ss.at[t, side],
             bulk_rs.at[t, side], device_id=peers[side], device_id_type=MESH,
         )
 
@@ -171,6 +143,14 @@
         return pltpu.make_async_remote_copy(
             bulk_s.at[t, side], bulk_r.at[t, side], bulk_ss.at[t, side],
             bulk_rs.at[t, side], device_id=peers[side], device_id_type=MESH,
+        )
+
+    def last_part(part, side):
+        at = pl.ds(part * PART, PART)
+        t = STEPS - 1
+        return pltpu.make_async_remote_copy(
+            bulk_s.at[t, side, at], bulk_r.at[t, side, at], last_ss.at[part, side],
+            last_rs.at[part, side], device_id=peers[side], device_id_type=MESH,
         )
 
     def flux(t, side):
@@ -202,32 +182,66 @@
     zero = jnp.zeros((8, LANES), F32)
 
     def send_flux(t, side, totals):
-        for i, total in enumerate(totals):
-            flux_s[t, side, i] = total
-        if len(totals) == 2:
-            flux_s[t, side, 2] = zero
-            flux_s[t, side, 3] = zero
+        rows = [jnp.sum(total, axis=0, keepdims=True) for total in totals]
+        rows += [jnp.zeros((1, LANES), F32)] * (4 - len(rows))
+        flux_s[t, side] = jnp.concatenate(rows, axis=0)
         pl.when(sends[side])(flux(t, side).start)
 
-    def first_group(c, carry):
+    def first(kk, carry, early=False):
+        pl.when(kk + AHEAD < HALF)(lambda: e_start(kk + AHEAD))
         out = []
         for side in range(2):
             for half in range(2):
-                e_load(c, side, half).wait()
-            totals = carry[2 * side : 2 * side + 2]
-            totals = lax.fori_loop(
-                0, GROUP, lambda i, s, side=side: pack(0, side, c * GROUP + i, s, None), totals
-            )
-            pl.when(sends[side] & (c < EARLY))(bulk(0, side, c).start)
-            out += list(totals)
+                e_load(kk, side, half).wait()
+            out += list(pack(0, side, kk, carry[2 * side : 2 * side + 2], None))
+            if early:
+                pl.when(sends[side])(bulk(0, side, kk).start)
         return tuple(out)
 
-    fluxes = lax.fori_loop(0, GROUPS, first_group, (zero,) * 4)
+    for load in loads[:2]:
+        load.wait()
+    fluxes = lax.fori_loop(0, 4, functools.partial(first, early=True), (zero,) * 4)
+
+    for load in loads[2:4]:
+        load.wait()
+    wind = breeze_v[...]
+    east, north = wind[0:1, :], wind[1:2, :]
+    factor = 0.4 / jnp.log(10.0 / drag_v[...])
+    factor = factor * factor
+    speed = jnp.sqrt(east * east + north * north + 1.0)
+    for h in range(4):
+        cut = slice(h * LANES, (h + 1) * LANES)
+        push = 1.2 * factor[:, cut] * speed[:, cut]
+        atm_s[4 * h : 4 * h + 1, :] = push * east[:, cut]
+        atm_s[4 * h + 1 : 4 * h + 2, :] = push * north[:, cut]
+        atm_s[4 * h + 2 : 4 * h + 3, :] = east[:, cut]
+        atm_s[4 * h + 3 : 4 * h + 4, :] = north[:, cut]
+
+    atm_copy = misc(atm_s, atm_r, 0, up_id)
+    pl.when(sends[0])(atm_copy.start)
+
+    fluxes = lax.fori_loop(4, EARLY, functools.partial(first, early=True), fluxes)
+    fluxes = lax.fori_loop(EARLY, HALF, first, fluxes)
     for side in range(2):
         send_flux(0, side, fluxes[2 * side : 2 * side + 2])
-    for c in range(EARLY, GROUPS):
+
+    @pl.loop(EARLY, HALF)
+    def _(kk):
         for side in range(2):
-            pl.when(sends[side])(bulk(0, side, c).start)
+            pl.when(sends[side])(bulk(0, side, kk).start)
+
+    for load in loads[4:9]:
+        load.wait()
+    ocean_mask = marine_v[...].astype(F32)
+    own_fields = [flow_v[0], flow_v[1], skin_v[...], ocean_mask, subs_v[...]]
+    for i, value in enumerate(own_fields):
+        sea_s[0, 4 * i : 4 * i + 4, :] = value[4:8, :]
+        sea_s[1, 4 * i : 4 * i + 4, :] = value[0:4, :]
+        ocean[i, 4:12, :] = value
+
+    sea_copies = [misc(sea_s.at[i], sea_r.at[i], 1 + i, peers[i]) for i in range(2)]
+    for side in range(2):
+        pl.when(sends[side])(sea_copies[side].start)
 
     for load in loads[9:]:
         load.wait()
@@ -283,10 +297,13 @@
         forcing.append(halves)
         for h in range(2):
             cut = slice(h * LANES, (h + 1) * LANES)
-            frc_s[0, 4 * i : 4 * i + 4, cut] = halves[h][4:8, :]
-            frc_s[1, 4 * i : 4 * i + 4, cut] = halves[h][0:4, :]
             if i < 2:
+                frc_s[0, 3 * i : 3 * i + 3, cut] = halves[h][5:8, :]
+                frc_s[1, 3 * i : 3 * i + 3, cut] = halves[h][0:3, :]
                 ocean[5 + i, 4:12, cut] = halves[h]
+            else:
+                frc_s[0, 4 + i : 5 + i, cut] = halves[h][7:8, :]
+                frc_s[1, 4 + i : 5 + i, cut] = halves[h][0:1, :]
     frc_copies = [misc(frc_s.at[i], frc_r.at[i], 3 + i, peers[i]) for i in range(2)]
     for side in range(2):
         pl.when(sends[side])(frc_copies[side].start)
@@ -354,7 +371,7 @@
         arrived = []
         for side in range(2):
             arrived.append(
-                [spread(jnp.sum(flux_r[t, side, i], axis=0, keepdims=True)) for i in range(4)]
+                [spread(flux_r[t, side, i : i + 1, :]) for i in range(4)]
             )
         for h in range(2):
             energy = sums[h] + jnp.where(row8 == 0, arrived[0][h], 0.0)
@@ -367,64 +384,64 @@
     def grow(t, neighbours):
         last = t == STEPS - 1
 
-        def group(c, carry):
+        def one(kk, carry):
             out = []
             for side in range(2):
-                def one(i, totals, side=side):
-                    kk = c * GROUP + i
-                    k = side * HALF + kk
-                    cosine, sine = dirs[4 * k], dirs[4 * k + 1]
-                    along = [cosine * state[0, h] + sine * state[1, h] for h in range(2)]
-                    kept = [state[2, h] for h in range(2)]
-                    base = [state[3, h] for h in range(2)]
-                    totals = list(totals)
-                    for m in range(NFREQ):
-                        rows = pl.ds(pl.multiple_of(k * 256 + m * 8, 8), 8)
-                        for h in range(2):
-                            grown = jnp.maximum(along[h] * float(INV_SPEED[m]) + base[h], kept[h])
-                            value = states[h][rows, :] * grown
-                            if last:
-                                p = 2 * (m % 2) + h
-                                totals[p] = totals[p] + value
-                                value = value * float(1.0 / WIDTH[m])
-                            states[h][rows, :] = value
-                    if last:
-                        return tuple(totals)
-                    return pack(t + 1, side, kk, totals, neighbours[side] if neighbours else None)
-
-                if last:
-                    carry = lax.fori_loop(0, GROUP, one, carry)
-                else:
-                    size = len(carry) // 2
-                    totals = lax.fori_loop(0, GROUP, one, carry[size * side : size * side + size])
-                    out += list(totals)
-            return carry if last else tuple(out)
-
-        return lax.fori_loop(0, GROUPS, group, (zero,) * (8 if neighbours else 4))
+                k = side * HALF + kk
+                cosine, sine = dirs[4 * k], dirs[4 * k + 1]
+                along = [cosine * state[0, h] + sine * state[1, h] for h in range(2)]
+                kept = [state[2, h] for h in range(2)]
+                base = [state[3, h] for h in range(2)]
+                size = len(carry) // 2
+                totals = list(carry[size * side : size * side + size])
+                for m in range(NFREQ):
+                    rows = pl.ds(pl.multiple_of(k * 256 + m * 8, 8), 8)
+                    for h in range(2):
+                        grown = jnp.maximum(along[h] * float(INV_SPEED[m]) + base[h], kept[h])
+                        value = states[h][rows, :] * grown
+                        if last:
+                            totals[h] = totals[h] + value
+                            value = value * float(1.0 / WIDTH[m])
+                        states[h][rows, :] = value
+                if not last:
+                    totals = pack(t + 1, side, kk, totals, neighbours[side] if neighbours else None)
+                out += list(totals)
+            return tuple(out)
+
+        return lax.fori_loop(0, HALF, one, (zero,) * (8 if neighbours else 4))
 
     def enter(t):
         last = t == STEPS - 1
         coef = 2 if t == 0 else (3 if last else 0)
-        for side in range(2):
+        def one(kk, carry, side):
             edge = 0 if side == 0 else 7
-            def one(kk, carry, side=side, edge=edge):
-                k = side * HALF + kk
-                sine = dirs[4 * k + 3]
-                rows = [[spread(state[i, h, edge : edge + 1, :]) for h in range(2)] for i in range(4)]
-                along = [dirs[4 * k] * rows[0][h] + dirs[4 * k + 1] * rows[1][h] for h in range(2)]
-                for g in range(NFREQ // 8):
-                    part = slice(8 * g, 8 * g + 8)
-                    weight = freq[coef, part, :] * sine
-                    for h in range(2):
-                        grown = jnp.maximum(along[h] * freq[1, part, :] + rows[3][h], rows[2][h])
-                        at = pl.ds(k * 256 + 64 * g + edge, 8, stride=8)
-                        states[h][at, :] = states[h][at, :] + bulk_r[t, side, kk, h, part, :] * weight * grown
-                return carry
-
-            @pl.when(receives[side])
-            def _():
-                bulk_all(t, side).wait_recv()
-                lax.fori_loop(0, HALF, one, 0)
+            k = side * HALF + kk
+            sine = dirs[4 * k + 3]
+            rows = [[spread(state[i, h, edge : edge + 1, :]) for h in range(2)] for i in range(4)]
+            along = [dirs[4 * k] * rows[0][h] + dirs[4 * k + 1] * rows[1][h] for h in range(2)]
+            for g in range(NFREQ // 8):
+                part = slice(8 * g, 8 * g + 8)
+                weight = freq[coef, part, :] * sine
+                for h in range(2):
+                    grown = jnp.maximum(along[h] * freq[1, part, :] + rows[3][h], rows[2][h])
+                    at = pl.ds(k * 256 + 64 * g + edge, 8, stride=8)
+                    states[h][at, :] = states[h][at, :] + bulk_r[t, side, kk, h, part, :] * weight * grown
+            return carry
+
+        size = PART if last else HALF
+
+        def arrive(part, carry):
+            for side in range(2):
+                @pl.when(receives[side])
+                def _(side=side):
+                    (last_part(part, side) if last else bulk_all(t, side)).wait_recv()
+                    lax.fori_loop(part * size, part * size + size, functools.partial(one, side=side), 0)
+            return carry
+
+        if last:
+            lax.fori_loop(0, HALF // PART, arrive, 0)
+        else:
+            arrive(0, 0)
 
     def run_ocean():
         for side in range(2):
@@ -434,7 +451,10 @@
             for i in range(5):
                 ocean[i, first : first + 4, :] = sea_r[side, 4 * i : 4 * i + 4, :]
             for i in range(2):
-                ocean[5 + i, first : first + 4, :] = frc_r[side, 4 * i : 4 * i + 4, :]
+                inner_row = first + 1 if side == 0 else first
+                ocean[5 + i, inner_row : inner_row + 3, :] = frc_r[side, 3 * i : 3 * i + 3, :]
+                outer_row = first if side == 0 else first + 3
+                ocean[5 + i, outer_row : outer_row + 1, :] = jnp.zeros((1, 2 * LANES), F32)
         u, v, q = ocean[0], ocean[1], ocean[2]
         wet, deep, push_u, push_v = ocean[3], ocean[4], ocean[5], ocean[6]
         rub = 0.05 * (jnp.sqrt(push_u * push_u + push_v * push_v + 0.01) / 1.2)
@@ -464,11 +484,11 @@
         neighbours = None
         if t == STEPS - 2:
             neighbours = []
-            for side, row in ((0, 0), (1, 3)):
+            for side in range(2):
                 other = 1 - side
                 neighbours.append(
                     [
-                        [0.01 * spread(frc_r[other, 4 * i + row : 4 * i + row + 1, cut]) for cut in cuts]
+                        [0.01 * spread(frc_r[other, 4 + i : 5 + i, cut]) for cut in cuts]
                         for i in (2, 3)
                     ]
                 )
@@ -478,7 +498,11 @@
             for side in range(2):
                 send_flux(t + 1, side, fluxes[size * side : size * side + size])
             for side in range(2):
-                pl.when(sends[side])(bulk_all(t + 1, side).start)
+                if t + 1 < STEPS - 1:
+                    pl.when(sends[side])(bulk_all(t + 1, side).start)
+                else:
+                    for part in range(HALF // PART):
+                        pl.when(sends[side])(last_part(part, side).start)
             enter(t)
 
     for h in range(2):
@@ -539,8 +563,11 @@
             for copy in ((atm_copy, sum_copy)[side], sea_copies[side], frc_copies[side]):
                 copy.wait_send()
             for t in range(STEPS):
-                bulk_all(t, side).wait_send()
+                if t < STEPS - 1:
+                    bulk_all(t, side).wait_send()
                 flux(t, side).wait_send()
+            for part in range(HALF // PART):
+                last_part(part, side).wait_send()
 
 
 def write_kernel(el, eh, cur, sst, drag, heat, e_out, cur_out, sst_out, drag_out, heat_out, sems):
@@ -585,17 +612,18 @@
             vmem((4, NFREQ, LANES), F32),
             vmem((STEPS, 2, HALF, 2, NFREQ, LANES), F32),
             vmem((STEPS, 2, HALF, 2, NFREQ, LANES), F32),
-            vmem((STEPS, 2, 4, 8, LANES), F32), vmem((STEPS, 2, 4, 8, LANES), F32),
+            vmem((STEPS, 2, 4, LANES), F32), vmem((STEPS, 2, 4, LANES), F32),
             vmem((16, LANES), F32), vmem((16, LANES), F32),
             vmem((2, 20, columns), F32), vmem((2, 20, columns), F32),
-            vmem((2, 16, columns), F32), vmem((2, 16, columns), F32),
+            vmem((2, 8, columns), F32), vmem((2, 8, columns), F32),
             vmem((16, LANES), F32), vmem((16, LANES), F32),
             pltpu.SMEM((4 * NDIR,), F32), pltpu.SMEM((1, 2), jnp.int32),
             vmem((LANES, LIST), BF16), vmem((LANES, LIST), BF16), vmem((1, LIST), F32),
             vmem((LANES, LANES), F32), vmem((7, 16, columns), F32), vmem((4, 2, 8, LANES), F32),
             vmem((LANES, LANES), F32),
-            dma((16,)), dma((GROUPS, 2, 2)),
-            dma((STEPS, 2)), dma((STEPS, 2)), dma((STEPS, 2)), dma((STEPS, 2)), dma((6,)), dma((6,)),
+            dma((16,)), dma((HALF, 2, 2)),
+            dma((STEPS - 1, 2)), dma((STEPS - 1, 2)), dma((HALF // PART, 2)), dma((HALF // PART, 2)),
+            dma((STEPS, 2)), dma((STEPS, 2)), dma((6,)), dma((6,)),
         ],
         compiler_params=pltpu.CompilerParams(
             collective_id=0, has_side_effects=True, vmem_limit_bytes=36 * 2**20

time: 69.1 us -> 66.2 us (0.958)
  Pallas kernels: 68.3 us -> 65.5 us
    pallas_call x1, Pallas kernels: 64.5 us -> 61.7 us  [per_device(): pl.pallas_call(functools.partial(main_kernel, axis_sizes), out_shape=[vme...]
where the time goes in v3:
time: 66.2 us; the launch traced here: 66.1 us
  Pallas kernels  65.5 us (99%)
    pallas_call x1, Pallas kernels, per_device(): pl.pallas_call(functools.partial(main_kernel, axis_sizes), out_shape=[vme...  61.7 us
    pallas_call x1, Pallas kernels, per_device(): pl.pallas_call(write_kernel, out_shape=[jax.ShapeDtypeStruct((lines, colu...  3.79 us

profile of v3, /device:TPU:24, one launch (start us, length us, event | category | flops | bytes accessed | tf_op | source)
XLA Modules:
  0.0 66.1 jit_solution(3232529000793537741)
XLA Ops:
  0.6 61.7 %coupled_step.1 = (f32[9216,128]{1,0:T(8,128)S(1)}, f32[9216,128]{1,0:T(8,128)S(1)}, f32[2,8,256]{2,1,0:T(8,128)S(1)}, f32[8,256]{1,0:T(8,128)S(1)}, f32[1,512]{1,0:T(1,128)S(1)}, /*index=5*/f32[1,512]{1,0:T(1,128)S(1)}) custom-call(f32[144]{0:T(256)} %constant.4.clone.dirs_in, s32[1,2]{1,0:T(1,128)} %tally_in.1, f32[9216,256]{1,0:T(8,128)} %bitcast.6, ...), custom_call_target="tpu_custom_call" | custom-call | tf_op jit(solution)/shard_map/coupled_step/pallas_call | solution.py:602
  62.3 3.8 %write_out.1 = (f32[9216,256]{1,0:T(8,128)}, f32[2,8,256]{2,1,0:T(8,128)}, f32[8,256]{1,0:T(8,128)}, f32[1,512]{1,0:T(1,128)}, f32[1,512]{1,0:T(1,128)}) custom-call(f32[9216,128]{1,0:T(8,128)S(1)} %get-tuple-element.16.el, f32[9216,128]{1,0:T(8,128)S(1)} %get-tuple-element.17.eh, f32[2,8,256]{2,1,0:T(8,128)S(1)} %get-tuple-element.18.cur, ...), custom_call_target="tpu_custom_call" | custom-call | tf_op jit(solution)/shard_map/write_out/pallas_call | solution.py:637

commit v4 on v3

--- a/solution.py
+++ b/solution.py
@@ -20,9 +20,11 @@
 EDGE = 384
 LIST = OWN + EDGE
 CHUNK = 512
-AHEAD = 6
+AHEAD = 10
 PART = 3
-EARLY = 9
+PARTS = HALF // PART
+EARLY = 2
+SOON = 2
 
 F32 = jnp.float32
 BF16 = jnp.bfloat16
@@ -60,14 +62,14 @@
 
 def main_kernel(
     axis_sizes,
-    dirs_in, tally_in, e_in, breeze, drag, heat, flow, skin, subs, marine,
+    dirs_in, tally_in, e_in, e_rows, breeze, drag, heat, flow, skin, subs, marine,
     own_src, own_tgt, own_w, edge_src, edge_tgt, edge_w, freq_in,
     el, eh, cur_out, sst_out, drag_out, heat_out,
     breeze_v, drag_v, heat_v, flow_v, skin_v, subs_v, marine_v,
     osrc_v, otgt_v, ow_v, esrc_v, etgt_v, ew_v, freq,
-    bulk_s, bulk_r, flux_s, flux_r, atm_s, atm_r, sea_s, sea_r, frc_s, frc_r, sum_s, sum_r,
+    first_r, bulk_s, bulk_r, flux_s, flux_r, atm_s, atm_r, sea_s, sea_r, frc_s, frc_r, sum_s, sum_r,
     dirs, tally, hot_src, hot_tgt, live_v, field, ocean, state, gather,
-    in_sem, e_sem, bulk_ss, bulk_rs, last_ss, last_rs, flux_ss, flux_rs, misc_ss, misc_rs,
+    in_sem, e_sem, bulk_ss, bulk_rs, flux_ss, flux_rs, misc_ss, misc_rs,
 ):
     mp, tile = lax.axis_index("mp"), lax.axis_index("tile")
     n_mp, n_tile = axis_sizes
@@ -133,25 +135,24 @@
     inner = (me > 0) & (me < count - 1)
     pl.semaphore_wait(barrier, jnp.where(inner, 2, 1).astype(jnp.int32))
 
-    def bulk(t, side, kk):
+    def moving(t, part, side):
+        at = pl.ds(part * PART, PART)
+        if t == 0:
+            src = e_rows.at[pl.ds(side * HALF + part * PART, PART), :, :, 7 if side == 0 else 0]
+            dst = first_r.at[side, at]
+        else:
+            src, dst = bulk_s.at[t - 1, side, at], bulk_r.at[t - 1, side, at]
         return pltpu.make_async_remote_copy(
-            bulk_s.at[t, side, kk], bulk_r.at[t, side, kk], bulk_ss.at[t, side],
-            bulk_rs.at[t, side], device_id=peers[side], device_id_type=MESH,
-        )
-
-    def bulk_all(t, side):
-        return pltpu.make_async_remote_copy(
-            bulk_s.at[t, side], bulk_r.at[t, side], bulk_ss.at[t, side],
-            bulk_rs.at[t, side], device_id=peers[side], device_id_type=MESH,
-        )
-
-    def last_part(part, side):
-        at = pl.ds(part * PART, PART)
-        t = STEPS - 1
-        return pltpu.make_async_remote_copy(
-            bulk_s.at[t, side, at], bulk_r.at[t, side, at], last_ss.at[part, side],
-            last_rs.at[part, side], device_id=peers[side], device_id_type=MESH,
-        )
+            src, dst, bulk_ss.at[t, part, side], bulk_rs.at[t, part, side],
+            device_id=peers[side], device_id_type=MESH,
+        )
+
+    def move(t, start, stop):
+        for part in range(start, stop):
+            for side in range(2):
+                pl.when(sends[side])(moving(t, part, side).start)
+
+    move(0, 0, 1)
 
     def flux(t, side):
         return pltpu.make_async_remote_copy(
@@ -171,7 +172,8 @@
             for h in range(2):
                 start = k * 256 + 64 * g + (7 if side == 0 else 0)
                 rows = states[h][pl.ds(start, 8, stride=8), :]
-                bulk_s[t, side, kk, h, 8 * g : 8 * g + 8, :] = rows
+                if t > 0:
+                    bulk_s[t - 1, side, kk, h, 8 * g : 8 * g + 8, :] = rows
                 moved = rows * weight
                 out[h] = out[h] + moved
                 if neighbour is not None:
@@ -187,20 +189,14 @@
         flux_s[t, side] = jnp.concatenate(rows, axis=0)
         pl.when(sends[side])(flux(t, side).start)
 
-    def first(kk, carry, early=False):
+    def first(kk, carry):
         pl.when(kk + AHEAD < HALF)(lambda: e_start(kk + AHEAD))
         out = []
         for side in range(2):
             for half in range(2):
                 e_load(kk, side, half).wait()
             out += list(pack(0, side, kk, carry[2 * side : 2 * side + 2], None))
-            if early:
-                pl.when(sends[side])(bulk(0, side, kk).start)
         return tuple(out)
-
-    for load in loads[:2]:
-        load.wait()
-    fluxes = lax.fori_loop(0, 4, functools.partial(first, early=True), (zero,) * 4)
 
     for load in loads[2:4]:
         load.wait()
@@ -219,16 +215,15 @@
 
     atm_copy = misc(atm_s, atm_r, 0, up_id)
     pl.when(sends[0])(atm_copy.start)
-
-    fluxes = lax.fori_loop(4, EARLY, functools.partial(first, early=True), fluxes)
-    fluxes = lax.fori_loop(EARLY, HALF, first, fluxes)
+    move(0, 1, EARLY)
+
+    for load in loads[:2]:
+        load.wait()
+    fluxes = lax.fori_loop(0, HALF, first, (zero,) * 4)
     for side in range(2):
         send_flux(0, side, fluxes[2 * side : 2 * side + 2])
 
-    @pl.loop(EARLY, HALF)
-    def _(kk):
-        for side in range(2):
-            pl.when(sends[side])(bulk(0, side, kk).start)
+    move(0, EARLY, PARTS)
 
     for load in loads[4:9]:
         load.wait()
@@ -281,54 +276,44 @@
             offset, CHUNK, osrc_v[:, at], otgt_v[:, at], ow_v[:, at], tally[0, 1] - offset, own_table
         )
 
-    total = lax.fori_loop(0, OWN // CHUNK, own_chunk, jnp.zeros((LANES, LANES), F32))
-    pl.when(receives[0])(atm_copy.wait_recv)
-    edge_limit = jnp.where(me > 0, tally[0, 0], 0)
-    total = total + to_fine(
-        OWN, EDGE, esrc_v[...], etgt_v[...], ew_v[...], edge_limit, two_parts(atm_r[...])
-    )
-    field[...] = total
-    forcing = []
-    for i in range(4):
-        halves = []
-        for h in range(2):
-            coarse = field[pl.ds(8 * h + i, 8, stride=16), :]
-            halves.append(coarse + field[pl.ds(8 * h + i + 4, 8, stride=16), :])
-        forcing.append(halves)
-        for h in range(2):
-            cut = slice(h * LANES, (h + 1) * LANES)
-            if i < 2:
-                frc_s[0, 3 * i : 3 * i + 3, cut] = halves[h][5:8, :]
-                frc_s[1, 3 * i : 3 * i + 3, cut] = halves[h][0:3, :]
-                ocean[5 + i, 4:12, cut] = halves[h]
-            else:
-                frc_s[0, 4 + i : 5 + i, cut] = halves[h][7:8, :]
-                frc_s[1, 4 + i : 5 + i, cut] = halves[h][0:1, :]
-    frc_copies = [misc(frc_s.at[i], frc_r.at[i], 3 + i, peers[i]) for i in range(2)]
-    for side in range(2):
-        pl.when(sends[side])(frc_copies[side].start)
-
-    cuts = [slice(0, LANES), slice(LANES, 2 * LANES)]
-    masks = [ocean_mask[:, cut] for cut in cuts]
-    friction = [
-        jnp.sqrt(forcing[0][h] * forcing[0][h] + forcing[1][h] * forcing[1][h] + 0.01) / 1.2
-        for h in range(2)
-    ]
-    for h in range(2):
-        state[0, h] = 0.01 * masks[h] * forcing[2][h]
-        state[1, h] = 0.01 * masks[h] * forcing[3][h]
-
     row8 = iota((8, LANES), 0)
     lane8 = iota((8, LANES), 1)
 
+    def enter(t, part):
+        last = t == STEPS - 1
+        coef = 2 if t == 0 else (3 if last else 0)
+        def one(kk, carry, side):
+            edge = 0 if side == 0 else 7
+            k = side * HALF + kk
+            sine = dirs[4 * k + 3]
+            rows = [[spread(state[i, h, edge : edge + 1, :]) for h in range(2)] for i in range(4)]
+            along = [dirs[4 * k] * rows[0][h] + dirs[4 * k + 1] * rows[1][h] for h in range(2)]
+            for g in range(NFREQ // 8):
+                cut = slice(8 * g, 8 * g + 8)
+                weight = freq[coef, cut, :] * sine
+                for h in range(2):
+                    grown = jnp.maximum(along[h] * freq[1, cut, :] + rows[3][h], rows[2][h])
+                    at = pl.ds(k * 256 + 64 * g + edge, 8, stride=8)
+                    if t == 0:
+                        came = first_r[side, kk, cut, h, 0, :]
+                    else:
+                        came = bulk_r[t - 1, side, kk, h, cut, :]
+                    states[h][at, :] = states[h][at, :] + came * weight * grown
+            return carry
+
+        for side in range(2):
+            @pl.when(receives[side])
+            def _(side=side):
+                moving(t, part, side).wait_recv()
+                lax.fori_loop(part * PART, part * PART + PART, functools.partial(one, side=side), 0)
+
     def advect(t):
         sums = (zero,) * 4
-        for quadrant in range(4):
-            west = quadrant in (0, 3)
-            south = quadrant < 2
-
-            def one(kk, sums, west=west, south=south, quadrant=quadrant):
-                k = quadrant * 9 + kk
+        for pair in range(2):
+            def one(kk, sums, side, pair=pair):
+                west = side == pair
+                south = side == 0
+                k = side * HALF + kk
                 cosine, sine = dirs[4 * k + 2], dirs[4 * k + 3]
                 both = cosine + sine
                 if west:
@@ -362,7 +347,15 @@
                     sums[p + 1] = sums[p + 1] + a_h
                 return tuple(sums)
 
-            sums = lax.fori_loop(0, 9, one, sums)
+            def part(p, sums, pair=pair, one=one):
+                p = p + pair * (PARTS // 2)
+                if t > 0:
+                    enter(t - 1, p)
+                for side in range(2):
+                    sums = lax.fori_loop(p * PART, p * PART + PART, functools.partial(one, side=side), sums)
+                return sums
+
+            sums = lax.fori_loop(0, PARTS // 2, part, sums)
         return [sums[0] + sums[2], sums[1] + sums[3]]
 
     def source(t, sums):
@@ -408,40 +401,12 @@
                 out += list(totals)
             return tuple(out)
 
-        return lax.fori_loop(0, HALF, one, (zero,) * (8 if neighbours else 4))
-
-    def enter(t):
-        last = t == STEPS - 1
-        coef = 2 if t == 0 else (3 if last else 0)
-        def one(kk, carry, side):
-            edge = 0 if side == 0 else 7
-            k = side * HALF + kk
-            sine = dirs[4 * k + 3]
-            rows = [[spread(state[i, h, edge : edge + 1, :]) for h in range(2)] for i in range(4)]
-            along = [dirs[4 * k] * rows[0][h] + dirs[4 * k + 1] * rows[1][h] for h in range(2)]
-            for g in range(NFREQ // 8):
-                part = slice(8 * g, 8 * g + 8)
-                weight = freq[coef, part, :] * sine
-                for h in range(2):
-                    grown = jnp.maximum(along[h] * freq[1, part, :] + rows[3][h], rows[2][h])
-                    at = pl.ds(k * 256 + 64 * g + edge, 8, stride=8)
-                    states[h][at, :] = states[h][at, :] + bulk_r[t, side, kk, h, part, :] * weight * grown
-            return carry
-
-        size = PART if last else HALF
-
-        def arrive(part, carry):
-            for side in range(2):
-                @pl.when(receives[side])
-                def _(side=side):
-                    (last_part(part, side) if last else bulk_all(t, side)).wait_recv()
-                    lax.fori_loop(part * size, part * size + size, functools.partial(one, side=side), 0)
-            return carry
-
+        totals = (zero,) * (8 if neighbours else 4)
         if last:
-            lax.fori_loop(0, HALF // PART, arrive, 0)
-        else:
-            arrive(0, 0)
+            return lax.fori_loop(0, HALF, one, totals)
+        totals = lax.fori_loop(0, SOON * PART, one, totals)
+        move(t + 1, 0, SOON)
+        return lax.fori_loop(SOON * PART, HALF, one, totals)
 
     def run_ocean():
         for side in range(2):
@@ -476,8 +441,47 @@
         cur_out[1] = ocean[1, 4:12, :]
         sst_out[...] = ocean[2, 4:12, :]
 
+    total = lax.fori_loop(0, OWN // CHUNK, own_chunk, jnp.zeros((LANES, LANES), F32))
+    sums = advect(0)
+    pl.when(receives[0])(atm_copy.wait_recv)
+    edge_limit = jnp.where(me > 0, tally[0, 0], 0)
+    total = total + to_fine(
+        OWN, EDGE, esrc_v[...], etgt_v[...], ew_v[...], edge_limit, two_parts(atm_r[...])
+    )
+    field[...] = total
+    forcing = []
+    for i in range(4):
+        halves = []
+        for h in range(2):
+            coarse = field[pl.ds(8 * h + i, 8, stride=16), :]
+            halves.append(coarse + field[pl.ds(8 * h + i + 4, 8, stride=16), :])
+        forcing.append(halves)
+        for h in range(2):
+            cut = slice(h * LANES, (h + 1) * LANES)
+            if i < 2:
+                frc_s[0, 3 * i : 3 * i + 3, cut] = halves[h][5:8, :]
+                frc_s[1, 3 * i : 3 * i + 3, cut] = halves[h][0:3, :]
+                ocean[5 + i, 4:12, cut] = halves[h]
+            else:
+                frc_s[0, 4 + i : 5 + i, cut] = halves[h][7:8, :]
+                frc_s[1, 4 + i : 5 + i, cut] = halves[h][0:1, :]
+    frc_copies = [misc(frc_s.at[i], frc_r.at[i], 3 + i, peers[i]) for i in range(2)]
+    for side in range(2):
+        pl.when(sends[side])(frc_copies[side].start)
+
+    cuts = [slice(0, LANES), slice(LANES, 2 * LANES)]
+    masks = [ocean_mask[:, cut] for cut in cuts]
+    friction = [
+        jnp.sqrt(forcing[0][h] * forcing[0][h] + forcing[1][h] * forcing[1][h] + 0.01) / 1.2
+        for h in range(2)
+    ]
+    for h in range(2):
+        state[0, h] = 0.01 * masks[h] * forcing[2][h]
+        state[1, h] = 0.01 * masks[h] * forcing[3][h]
+
     for t in range(STEPS):
-        sums = advect(t)
+        if t > 0:
+            sums = advect(t)
         if t == STEPS - 2:
             run_ocean()
         arrived = source(t, sums)
@@ -497,13 +501,7 @@
             size = len(fluxes) // 2
             for side in range(2):
                 send_flux(t + 1, side, fluxes[size * side : size * side + size])
-            for side in range(2):
-                if t + 1 < STEPS - 1:
-                    pl.when(sends[side])(bulk_all(t + 1, side).start)
-                else:
-                    for part in range(HALF // PART):
-                        pl.when(sends[side])(last_part(part, side).start)
-            enter(t)
+            move(t + 1, SOON, PARTS)
 
     for h in range(2):
         energy = fluxes[h] + fluxes[2 + h]
@@ -547,7 +545,7 @@
 
     own_sums = joined(lax.fori_loop(0, OWN // CHUNK, back_chunk, jnp.zeros((32, LANES), F32)))
 
-    enter(STEPS - 1)
+    lax.fori_loop(0, PARTS, lambda part, carry: (enter(STEPS - 1, part), carry)[1], 0)
 
     pl.when(receives[1])(sum_copy.wait_recv)
     totals = own_sums + sum_r[...]
@@ -563,11 +561,9 @@
             for copy in ((atm_copy, sum_copy)[side], sea_copies[side], frc_copies[side]):
                 copy.wait_send()
             for t in range(STEPS):
-                if t < STEPS - 1:
-                    bulk_all(t, side).wait_send()
                 flux(t, side).wait_send()
-            for part in range(HALF // PART):
-                last_part(part, side).wait_send()
+                for part in range(PARTS):
+                    moving(t, part, side).wait_send()
 
 
 def write_kernel(el, eh, cur, sst, drag, heat, e_out, cur_out, sst_out, drag_out, heat_out, sems):
@@ -593,6 +589,8 @@
     ndir, nfreq, rows, columns = swell.shape
     cells = drag.shape[0]
     lines = ndir * nfreq * rows
+    rows_view = swell.reshape(ndir, nfreq, rows, 2, LANES).transpose(0, 1, 3, 2, 4)
+    rows_view = rows_view.reshape(ndir, nfreq, 2, rows, 1, LANES)
     swell = swell.reshape(lines, columns)
     hbm_spec = pl.BlockSpec(memory_space=pltpu.HBM)
     vmem_spec = pl.BlockSpec(memory_space=pltpu.VMEM)
@@ -602,7 +600,7 @@
     results = pl.pallas_call(
         functools.partial(main_kernel, axis_sizes),
         out_shape=[vmem((lines, LANES), F32)] * 2 + [vmem(s, d) for s, d in small_out],
-        in_specs=[hbm_spec] * 17,
+        in_specs=[hbm_spec] * 18,
         out_specs=[vmem_spec] * 6,
         scratch_shapes=[
             vmem(breeze.shape, F32), vmem((1, cells), F32), vmem((1, cells), F32), vmem(flow.shape, F32),
@@ -610,8 +608,9 @@
             vmem((1, OWN), jnp.int32), vmem((1, OWN), jnp.int32), vmem((1, OWN), F32),
             vmem((1, EDGE), jnp.int32), vmem((1, EDGE), jnp.int32), vmem((1, EDGE), F32),
             vmem((4, NFREQ, LANES), F32),
-            vmem((STEPS, 2, HALF, 2, NFREQ, LANES), F32),
-            vmem((STEPS, 2, HALF, 2, NFREQ, LANES), F32),
+            vmem((2, HALF, NFREQ, 2, 1, LANES), F32),
+            vmem((STEPS - 1, 2, HALF, 2, NFREQ, LANES), F32),
+            vmem((STEPS - 1, 2, HALF, 2, NFREQ, LANES), F32),
             vmem((STEPS, 2, 4, LANES), F32), vmem((STEPS, 2, 4, LANES), F32),
             vmem((16, LANES), F32), vmem((16, LANES), F32),
             vmem((2, 20, columns), F32), vmem((2, 20, columns), F32),
@@ -622,7 +621,7 @@
             vmem((LANES, LANES), F32), vmem((7, 16, columns), F32), vmem((4, 2, 8, LANES), F32),
             vmem((LANES, LANES), F32),
             dma((16,)), dma((HALF, 2, 2)),
-            dma((STEPS - 1, 2)), dma((STEPS - 1, 2)), dma((HALF // PART, 2)), dma((HALF // PART, 2)),
+            dma((STEPS, PARTS, 2)), dma((STEPS, PARTS, 2)),
             dma((STEPS, 2)), dma((STEPS, 2)), dma((6,)), dma((6,)),
         ],
         compiler_params=pltpu.CompilerParams(
@@ -630,7 +629,7 @@
         ),
         name="coupled_step",
     )(*(pltpu.with_memory_space_constraint(x, pltpu.HBM) for x in (
-        jnp.asarray(direction_table()), tally, swell, breeze, drag.reshape(1, cells), heat.reshape(1, cells),
+        jnp.asarray(direction_table()), tally, swell, rows_view, breeze, drag.reshape(1, cells), heat.reshape(1, cells),
         flow, skin, subs, marine, own_src, own_tgt, own_w, edge_src, edge_tgt, edge_w,
         jnp.asarray(frequency_table()),
     )))

time: 66.2 us -> 65.9 us (level)
  no operation moved by 1% of the time
where the time goes in v4:
time: 65.9 us; the launch traced here: 65.8 us
  Pallas kernels  65.1 us (99%)
    pallas_call x1, Pallas kernels, per_device(): pl.pallas_call(functools.partial(main_kernel, axis_sizes), out_shape=[vme...  61.4 us
    pallas_call x1, Pallas kernels, per_device(): pl.pallas_call(write_kernel, out_shape=[jax.ShapeDtypeStruct((lines, colu...  3.79 us

profile of v4, /device:TPU:24, one launch (start us, length us, event | category | flops | bytes accessed | tf_op | source)
XLA Modules:
  0.0 65.8 jit_solution(598937729251152623)
XLA Ops:
  0.6 61.4 %coupled_step.1 = (f32[9216,128]{1,0:T(8,128)S(1)}, f32[9216,128]{1,0:T(8,128)S(1)}, f32[2,8,256]{2,1,0:T(8,128)S(1)}, f32[8,256]{1,0:T(8,128)S(1)}, f32[1,512]{1,0:T(1,128)S(1)}, /*index=5*/f32[1,512]{1,0:T(1,128)S(1)}) custom-call(f32[144]{0:T(256)} %constant.4.clone.dirs_in, s32[1,2]{1,0:T(1,128)} %tally_in.1, f32[9216,256]{1,0:T(8,128)} %bitcast.11, ...), custom_call_target="tpu_custom_call" | custom-call | tf_op jit(solution)/shard_map/coupled_step/pallas_call | solution.py:600
  62.0 3.8 %write_out.1 = (f32[9216,256]{1,0:T(8,128)}, f32[2,8,256]{2,1,0:T(8,128)}, f32[8,256]{1,0:T(8,128)}, f32[1,512]{1,0:T(1,128)}, f32[1,512]{1,0:T(1,128)}) custom-call(f32[9216,128]{1,0:T(8,128)S(1)} %get-tuple-element.16.el, f32[9216,128]{1,0:T(8,128)S(1)} %get-tuple-element.17.eh, f32[2,8,256]{2,1,0:T(8,128)S(1)} %get-tuple-element.18.cur, ...), custom_call_target="tpu_custom_call" | custom-call | tf_op jit(solution)/shard_map/write_out/pallas_call | solution.py:636

commit v5 on v4

--- a/solution.py
+++ b/solution.py
@@ -24,7 +24,7 @@
 PART = 3
 PARTS = HALF // PART
 EARLY = 2
-SOON = 2
+SOON = 3
 
 F32 = jnp.float32
 BF16 = jnp.bfloat16

time: 65.9 us -> 68.4 us (1.038)
  Pallas kernels: 65.1 us -> 67.6 us
    pallas_call x1, Pallas kernels: 61.4 us -> 63.8 us  [per_device(): pl.pallas_call(functools.partial(main_kernel, axis_sizes), out_shape=[vme...]
where the time goes in v5:
time: 68.4 us; the launch traced here: 68.3 us
  Pallas kernels  67.6 us (99%)
    pallas_call x1, Pallas kernels, per_device(): pl.pallas_call(functools.partial(main_kernel, axis_sizes), out_shape=[vme...  63.8 us
    pallas_call x1, Pallas kernels, per_device(): pl.pallas_call(write_kernel, out_shape=[jax.ShapeDtypeStruct((lines, colu...  3.79 us

profile of v5, /device:TPU:24, one launch (start us, length us, event | category | flops | bytes accessed | tf_op | source)
XLA Modules:
  0.0 68.3 jit_solution(12323352702629437227)
XLA Ops:
  0.6 63.8 %coupled_step.1 = (f32[9216,128]{1,0:T(8,128)S(1)}, f32[9216,128]{1,0:T(8,128)S(1)}, f32[2,8,256]{2,1,0:T(8,128)S(1)}, f32[8,256]{1,0:T(8,128)S(1)}, f32[1,512]{1,0:T(1,128)S(1)}, /*index=5*/f32[1,512]{1,0:T(1,128)S(1)}) custom-call(f32[144]{0:T(256)} %constant.4.clone.dirs_in, s32[1,2]{1,0:T(1,128)} %tally_in.1, f32[9216,256]{1,0:T(8,128)} %bitcast.11, ...), custom_call_target="tpu_custom_call" | custom-call | tf_op jit(solution)/shard_map/coupled_step/pallas_call | solution.py:600
  64.5 3.8 %write_out.1 = (f32[9216,256]{1,0:T(8,128)}, f32[2,8,256]{2,1,0:T(8,128)}, f32[8,256]{1,0:T(8,128)}, f32[1,512]{1,0:T(1,128)}, f32[1,512]{1,0:T(1,128)}) custom-call(f32[9216,128]{1,0:T(8,128)S(1)} %get-tuple-element.16.el, f32[9216,128]{1,0:T(8,128)S(1)} %get-tuple-element.17.eh, f32[2,8,256]{2,1,0:T(8,128)S(1)} %get-tuple-element.18.cur, ...), custom_call_target="tpu_custom_call" | custom-call | tf_op jit(solution)/shard_map/write_out/pallas_call | solution.py:636
